TPU v7x, 32 devices: a whole 2x2x4 slice. The times are simulated.
32 devices in a mesh: wide: 16 (over z, y, x), narrow: 2 (over core).
Axes of the slice: x: 2, y: 2, z: 4, core: 2. Of those that a mesh axis runs over, the one named last changes fastest.
Arguments:
- frames: bfloat16 [16384, 1024], P(('wide', 'narrow')), may hold values from -6 to 6
- segment_ids: int32 [16, 1024], P('wide'), may hold values from 0 to 5, never falling along the last dimension, each value on 1 to 350 neighbouring positions
- w_query: bfloat16 [1024, 1024], P(None, 'narrow'), may hold values from -0.25 to 0.25
- w_key: bfloat16 [1024, 1024], P(None, 'narrow'), may hold values from -0.25 to 0.25
- w_value: bfloat16 [1024, 1024], P(None, 'narrow'), may hold values from -0.1875 to 0.1875
- w_out: bfloat16 [1024, 1024], P('narrow'), may hold values from -0.5 to 0.5
- w_gate: bfloat16 [1024, 4096], P(None, 'narrow'), may hold values from -0.1875 to 0.1875
- w_up: bfloat16 [1024, 4096], P(None, 'narrow'), may hold values from -0.1875 to 0.1875
- w_down: bfloat16 [4096, 1024], P('narrow'), may hold values from -0.09375 to 0.09375
- norm1_gain: float32 [1024], replicated, may hold values from 0.1 to 1.9
- norm1_bias: float32 [1024], replicated, may hold values from -3 to 3
- norm2_gain: float32 [1024], replicated, may hold values from 0.1 to 1.9
- norm2_bias: float32 [1024], replicated, may hold values from -3 to 3
- scale_attn: float32 [1024], replicated, may hold values from 0.5 to 1.5
- scale_mlp: float32 [1024], replicated, may hold values from 0.5 to 1.5
- output_grad: bfloat16 [16384, 1024], P(('wide', 'narrow')), may hold values from -6 to 6
Outputs:
- output: bfloat16 [16384, 1024], P(('wide', 'narrow'))
- input_grad: bfloat16 [16384, 1024], P(('wide', 'narrow'))
- query_grad: float32 [1024, 1024], P('wide', 'narrow')
- key_grad: float32 [1024, 1024], P('wide', 'narrow')
- value_grad: float32 [1024, 1024], P('wide', 'narrow')
- out_proj_grad: float32 [1024, 1024], P('narrow', 'wide')
- gate_grad: float32 [1024, 4096], P('wide', 'narrow')
- up_grad: float32 [1024, 4096], P('wide', 'narrow')
- down_grad: float32 [4096, 1024], P('narrow', 'wide')
- norm1_gain_grad: float32 [1024], replicated
- norm1_bias_grad: float32 [1024], replicated
- norm2_gain_grad: float32 [1024], replicated
- norm2_bias_grad: float32 [1024], replicated
- scale_attn_grad: float32 [1024], replicated
- scale_mlp_grad: float32 [1024], replicated
Inputs may be any that keep to these rules, and one draw needn't show every extreme that they name: `segment_ids`: along each sequence the clip numbers never fall, and a clip holds at most 350 frames.
All inputs are finite; a program needn't handle non-finite values.
Results may differ from a plain program's by a relative error of at most 0.023.
Values may be sent and summed in bfloat16 or wider, within the bound.
No kernel may reach another device: no remote copies, remote signals or barrier semaphores. Data moves between devices by JAX's collectives and lax.ppermute only.
A program may use at most 192 MiB of HBM per device.

v0:
```python
import math

import jax
import jax.numpy as jnp
from jax import lax
from jax.sharding import PartitionSpec as P

HEAD_DIM = 64
WINDOW = 128


norm_eps = 1e-05
masked_score = -1e30


def layer_norm(row_block, norm_gain, norm_shift):
    mean_row = jnp.mean(row_block, axis=-1, keepdims=True)
    centred = row_block - mean_row
    inverse = lax.rsqrt(jnp.mean(centred * centred, axis=-1, keepdims=True) + norm_eps)
    unit_rows = centred * inverse
    return (unit_rows * norm_gain + norm_shift, unit_rows, inverse)


def norm_back(incoming, unit_rows, inverse, norm_gain):
    scaled = incoming * norm_gain
    return inverse * (
        scaled
        - jnp.mean(scaled, axis=-1, keepdims=True)
        - unit_rows * jnp.mean(scaled * unit_rows, axis=-1, keepdims=True)
    )


def positions(segment_ids):
    place = lax.broadcasted_iota(jnp.int32, segment_ids.shape, 1)
    edges = jnp.concatenate(
        [
            jnp.ones_like(segment_ids[:, :1]),
            (segment_ids[:, 1:] != segment_ids[:, :-1]).astype(jnp.int32),
        ],
        axis=1,
    )
    starts = lax.cummax(jnp.where(edges == 1, place, 0), axis=1)
    return (place - starts).astype(jnp.float32)


def rotary_tables(where_in, half_size):
    frequency = jnp.exp(jnp.arange(half_size, dtype=jnp.float32) * (-math.log(10000.0) / half_size))
    angles = where_in.reshape(-1, 1) * frequency[None, :]
    return (jnp.cos(angles)[:, None, :], jnp.sin(angles)[:, None, :])


def rotate(vectors, cosine_table, sine_table):
    half_size = vectors.shape[-1] // 2
    front_half = vectors[..., :half_size]
    back_half = vectors[..., half_size:]
    return jnp.concatenate(
        [
            front_half * cosine_table - back_half * sine_table,
            front_half * sine_table + back_half * cosine_table,
        ],
        axis=-1,
    )


def rotate_back(incoming, cosine_table, sine_table):
    half_size = incoming.shape[-1] // 2
    front_half = incoming[..., :half_size]
    back_half = incoming[..., half_size:]
    return jnp.concatenate(
        [
            front_half * cosine_table + back_half * sine_table,
            back_half * cosine_table - front_half * sine_table,
        ],
        axis=-1,
    )


def row_contract(left_rows, right_rows):
    return lax.dot_general(
        left_rows, right_rows, (((0,), (0,)), ((), ())), preferred_element_type=jnp.float32
    )


def column_contract(left_rows, right_rows):
    return lax.dot_general(
        left_rows, right_rows, (((1,), (1,)), ((), ())), preferred_element_type=jnp.float32
    )


def reduce_forward(partial_sum):
    return lax.psum(partial_sum, "narrow")


def reduce_back(partial_sum):
    return lax.psum(partial_sum, "narrow")


def own_rows(row_block):
    share_count = row_block.shape[0] // lax.axis_size("narrow")
    return lax.dynamic_slice_in_dim(
        row_block, lax.axis_index("narrow") * share_count, share_count, 0
    )


def banding(query, key, value, segments, block_rows):
    sequences, length, head_count, head_size = query.shape
    half_window = WINDOW // 2
    padding = ((0, 0), (half_window, half_window), (0, 0), (0, 0))
    key_pad = jnp.pad(key, padding)
    value_pad = jnp.pad(value, padding)
    segment_pad = jnp.pad(segments, ((0, 0), (half_window, half_window)), constant_values=-1)
    per_sequence = length // block_rows
    score_scale = head_size ** (-0.5)
    span_rows = block_rows + WINDOW
    offset = lax.broadcasted_iota(jnp.int32, (block_rows, span_rows), 1) - lax.broadcasted_iota(
        jnp.int32, (block_rows, span_rows), 0
    )
    inside = (offset >= 0) & (offset < WINDOW)

    def cut_band(block_index):
        sequence = block_index // per_sequence
        start_row = block_index % per_sequence * block_rows
        query_rows = lax.dynamic_slice(
            query, (sequence, start_row, 0, 0), (1, block_rows, head_count, head_size)
        )[0]
        key_rows = lax.dynamic_slice(
            key_pad, (sequence, start_row, 0, 0), (1, span_rows, head_count, head_size)
        )[0]
        value_rows = lax.dynamic_slice(
            value_pad, (sequence, start_row, 0, 0), (1, span_rows, head_count, head_size)
        )[0]
        query_segment = lax.dynamic_slice(segments, (sequence, start_row), (1, block_rows))[0]
        key_segment = lax.dynamic_slice(segment_pad, (sequence, start_row), (1, span_rows))[0]
        allowed = inside & (query_segment[:, None] == key_segment[None, :])
        scores = (
            jnp.einsum("qhd,khd->hqk", query_rows, key_rows, preferred_element_type=jnp.float32)
            * score_scale
        )
        return (
            jnp.where(allowed[None], scores, masked_score),
            query_rows,
            key_rows,
            value_rows,
            sequence,
            start_row,
        )

    return cut_band


def attention_forward(cut_band, total_blocks):

    def forward_block(block_index):
        scores, query_rows, key_rows, value_rows, sequence, start_row = cut_band(block_index)
        row_top = jnp.max(scores, axis=-1, keepdims=True)
        lifted = jnp.exp(scores - row_top)
        row_total = jnp.sum(lifted, axis=-1, keepdims=True)
        weights = (lifted / row_total).astype(jnp.bfloat16)
        mixture = jnp.einsum(
            "hqk,khd->qhd", weights, value_rows, preferred_element_type=jnp.float32
        )
        return (mixture, (row_top + jnp.log(row_total))[..., 0])

    return lax.map(forward_block, jnp.arange(total_blocks, dtype=jnp.int32))


def attention_backward(cut_band, total_blocks, block_rows, logsum, mixture_grad):
    sequences, length, head_count, head_size = mixture_grad.shape
    score_scale = head_size ** (-0.5)
    span_rows = block_rows + WINDOW
    zero_state = jnp.zeros((sequences, length + WINDOW, head_count, head_size), jnp.float32)

    def back_block(accumulated, block_index):
        key_acc, value_acc = accumulated
        scores, query_rows, key_rows, value_rows, sequence, start_row = cut_band(block_index)
        grad_rows = lax.dynamic_slice(
            mixture_grad, (sequence, start_row, 0, 0), (1, block_rows, head_count, head_size)
        )[0]
        chances = jnp.exp(scores - logsum[block_index][:, :, None])
        chances_low = chances.astype(jnp.bfloat16)
        chance_grad = jnp.einsum(
            "qhd,khd->hqk", grad_rows, value_rows, preferred_element_type=jnp.float32
        )
        weighted = jnp.sum(chances * chance_grad, axis=-1, keepdims=True)
        score_grad = (chances * (chance_grad - weighted)).astype(jnp.bfloat16)
        query_part = (
            jnp.einsum("hqk,khd->qhd", score_grad, key_rows, preferred_element_type=jnp.float32)
            * score_scale
        )
        key_part = (
            jnp.einsum("hqk,qhd->khd", score_grad, query_rows, preferred_element_type=jnp.float32)
            * score_scale
        )
        value_part = jnp.einsum(
            "hqk,qhd->khd", chances_low, grad_rows, preferred_element_type=jnp.float32
        )
        corner = (sequence, start_row, 0, 0)
        window_shape = (1, span_rows, head_count, head_size)
        key_acc = lax.dynamic_update_slice(
            key_acc, lax.dynamic_slice(key_acc, corner, window_shape) + key_part[None], corner
        )
        value_acc = lax.dynamic_update_slice(
            value_acc, lax.dynamic_slice(value_acc, corner, window_shape) + value_part[None], corner
        )
        return ((key_acc, value_acc), query_part)

    sums_kept, query_parts = lax.scan(
        back_block, (zero_state, zero_state), jnp.arange(total_blocks, dtype=jnp.int32)
    )
    half_window = WINDOW // 2
    key_total = sums_kept[0][:, half_window : half_window + length]
    value_total = sums_kept[1][:, half_window : half_window + length]
    flat_shape = (sequences * length, head_count, head_size)
    return (
        query_parts.reshape(flat_shape),
        key_total.reshape(flat_shape),
        value_total.reshape(flat_shape),
    )


def on_device(
    frames,
    segment_ids,
    w_query,
    w_key,
    w_value,
    w_out,
    w_gate,
    w_up,
    w_down,
    norm1_gain,
    norm1_bias,
    norm2_gain,
    norm2_bias,
    scale_attn,
    scale_mlp,
    output_grad,
):
    gathered = (
        lax.all_gather(frames, "narrow", axis=0, tiled=True),
        lax.all_gather(output_grad, "narrow", axis=0, tiled=True),
    )
    inputs = gathered[0].astype(jnp.float32)
    cotangent = gathered[1].astype(jnp.float32)
    sequences, length = segment_ids.shape
    head_size = HEAD_DIM
    local_heads = w_query.shape[1] // head_size
    block_rows = min(512, length)
    total_blocks = sequences * length // block_rows
    cosine_table, sine_table = rotary_tables(positions(segment_ids), head_size // 2)
    normed_one, unit_one, inverse_one = layer_norm(inputs, norm1_gain, norm1_bias)
    attn_in = normed_one.astype(jnp.bfloat16)
    row_count = attn_in.shape[0]
    shape_four = (sequences, length, local_heads, head_size)

    def heads_of(matrix):
        return matrix.reshape(row_count, local_heads, head_size)

    query_rot = rotate(
        heads_of(jnp.dot(attn_in, w_query, preferred_element_type=jnp.float32)),
        cosine_table,
        sine_table,
    ).astype(jnp.bfloat16)
    key_rot = rotate(
        heads_of(jnp.dot(attn_in, w_key, preferred_element_type=jnp.float32)),
        cosine_table,
        sine_table,
    ).astype(jnp.bfloat16)
    value_rows = heads_of(
        jnp.dot(attn_in, w_value, preferred_element_type=jnp.float32).astype(jnp.bfloat16)
    )
    cut_band = banding(
        query_rot.reshape(shape_four),
        key_rot.reshape(shape_four),
        value_rows.reshape(shape_four),
        segment_ids,
        block_rows,
    )
    mixture, logsum = attention_forward(cut_band, total_blocks)
    mixture_low = mixture.reshape(row_count, local_heads * head_size).astype(jnp.bfloat16)
    attn_out = reduce_forward(jnp.dot(mixture_low, w_out, preferred_element_type=jnp.float32))
    middle = inputs + scale_attn * attn_out
    normed_two, unit_two, inverse_two = layer_norm(middle, norm2_gain, norm2_bias)
    mlp_in = normed_two.astype(jnp.bfloat16)
    gate_pre = jnp.dot(mlp_in, w_gate, preferred_element_type=jnp.float32)
    up_pre = jnp.dot(mlp_in, w_up, preferred_element_type=jnp.float32)
    gate_sigmoid = jax.nn.sigmoid(gate_pre)
    activated = gate_pre * gate_sigmoid
    hidden = (activated * up_pre).astype(jnp.bfloat16)
    mlp_out = reduce_forward(jnp.dot(hidden, w_down, preferred_element_type=jnp.float32))
    result = middle + scale_mlp * mlp_out
    output = own_rows(result).astype(jnp.bfloat16)
    mlp_grad = (scale_mlp * cotangent).astype(jnp.bfloat16)
    hidden_back = column_contract(mlp_grad, w_down)
    down_part = row_contract(hidden, mlp_grad)
    gate_back = (
        hidden_back * up_pre * gate_sigmoid * (1.0 + gate_pre * (1.0 - gate_sigmoid))
    ).astype(jnp.bfloat16)
    up_back = (hidden_back * activated).astype(jnp.bfloat16)
    mlp_weights = (
        lax.psum_scatter(
            row_contract(mlp_in, gate_back).astype(jnp.bfloat16),
            "wide",
            scatter_dimension=0,
            tiled=True,
        ).astype(jnp.float32),
        lax.psum_scatter(
            row_contract(mlp_in, up_back).astype(jnp.bfloat16),
            "wide",
            scatter_dimension=0,
            tiled=True,
        ).astype(jnp.float32),
        lax.psum_scatter(
            down_part.astype(jnp.bfloat16), "wide", scatter_dimension=1, tiled=True
        ).astype(jnp.float32),
    )
    norm_two_grad = reduce_back(column_contract(gate_back, w_gate) + column_contract(up_back, w_up))
    middle_grad = cotangent + norm_back(norm_two_grad, unit_two, inverse_two, norm2_gain)
    attn_grad = (scale_attn * middle_grad).astype(jnp.bfloat16)
    proj_part = row_contract(mixture_low, attn_grad)
    mixture_grad = column_contract(attn_grad, w_out).astype(jnp.bfloat16)
    query_back, key_back, value_back = attention_backward(
        cut_band, total_blocks, block_rows, logsum, mixture_grad.reshape(shape_four)
    )
    query_pre_grad = (
        rotate_back(query_back, cosine_table, sine_table)
        .reshape(row_count, -1)
        .astype(jnp.bfloat16)
    )
    key_pre_grad = (
        rotate_back(key_back, cosine_table, sine_table).reshape(row_count, -1).astype(jnp.bfloat16)
    )
    value_pre_grad = value_back.reshape(row_count, -1).astype(jnp.bfloat16)
    attn_weights = (
        lax.psum_scatter(
            row_contract(attn_in, query_pre_grad).astype(jnp.bfloat16),
            "wide",
            scatter_dimension=0,
            tiled=True,
        ).astype(jnp.float32),
        lax.psum_scatter(
            row_contract(attn_in, key_pre_grad).astype(jnp.bfloat16),
            "wide",
            scatter_dimension=0,
            tiled=True,
        ).astype(jnp.float32),
        lax.psum_scatter(
            row_contract(attn_in, value_pre_grad).astype(jnp.bfloat16),
            "wide",
            scatter_dimension=0,
            tiled=True,
        ).astype(jnp.float32),
        lax.psum_scatter(
            proj_part.astype(jnp.bfloat16), "wide", scatter_dimension=1, tiled=True
        ).astype(jnp.float32),
    )
    norm_one_grad = reduce_back(
        column_contract(query_pre_grad, w_query)
        + column_contract(key_pre_grad, w_key)
        + column_contract(value_pre_grad, w_value)
    )
    input_full = middle_grad + norm_back(norm_one_grad, unit_one, inverse_one, norm1_gain)
    input_grad = own_rows(input_full).astype(jnp.bfloat16)
    own_one_grad = own_rows(norm_one_grad)
    own_two_grad = own_rows(norm_two_grad)
    vector_grads = lax.psum(
        (
            jnp.sum(own_one_grad * own_rows(unit_one), axis=0),
            jnp.sum(own_one_grad, axis=0),
            jnp.sum(own_two_grad * own_rows(unit_two), axis=0),
            jnp.sum(own_two_grad, axis=0),
            jnp.sum(own_rows(attn_out) * own_rows(middle_grad), axis=0),
            jnp.sum(own_rows(mlp_out) * own_rows(cotangent), axis=0),
        ),
        ("wide", "narrow"),
    )
    return (
        output,
        input_grad,
        attn_weights[0],
        attn_weights[1],
        attn_weights[2],
        attn_weights[3],
        mlp_weights[0],
        mlp_weights[1],
        mlp_weights[2],
        vector_grads[0],
        vector_grads[1],
        vector_grads[2],
        vector_grads[3],
        vector_grads[4],
        vector_grads[5],
    )


def solution(mesh):
    return jax.shard_map(
        on_device,
        mesh=mesh,
        in_specs=(
            P(("wide", "narrow"), None),
            P("wide", None),
            P(None, "narrow"),
            P(None, "narrow"),
            P(None, "narrow"),
            P("narrow", None),
            P(None, "narrow"),
            P(None, "narrow"),
            P("narrow", None),
            P(),
            P(),
            P(),
            P(),
            P(),
            P(),
            P(("wide", "narrow"), None),
        ),
        out_specs=(
            P(("wide", "narrow"), None),
            P(("wide", "narrow"), None),
            P("wide", "narrow"),
            P("wide", "narrow"),
            P("wide", "narrow"),
            P("narrow", "wide"),
            P("wide", "narrow"),
            P("wide", "narrow"),
            P("narrow", "wide"),
            P(),
            P(),
            P(),
            P(),
            P(),
            P(),
        ),
        check_vma=False,
    )
```

profile of v0, /device:TPU:0, one launch (start us, length us, event | category | flops | bytes accessed | tf_op | source)
XLA Modules:
  0.0 919.8 jit_solution(6625966685127138778)
XLA Ops:
  11.1 11.8 %all-gather.3.cloned.1.call-done = bf16[1024,1024]{1,0:T(8,128)(2,1)} async-done(((bf16[512,1024]{1,0:T(8,128)(2,1)}), bf16[1024,1024]{1,0:T(8,128)(2,1)}) %all-gather.3.cloned.1.call-update) | async-done | bytes 2097168 | tf_op jit(solution)/shard_map/all_gather | solution.py:240
  38.2 25.0 %while.32 = (s32[]{:T(128)}, bf16[2,512,8,64]{1,3,2,0:T(8,128)(2,1)}, f32[2,8,512]{2,1,0:T(8,128)S(1)}, s32[2]{0:T(128)S(1)}, bf16[1,1152,8,64]{1,3,2,0:T(8,128)...) while((s32[]{:T(128)}, ...), condition=%wide.region_7.8_spmd.clone, body=%wide.region_4.7_spmd.clone.sunk | while | flops 704507904 | bytes 48904132 | solution.py:164
  70.8 28.9 %all-reduce.9.cloned.1.call-done = f32[1024,1024]{1,0:T(8,128)} async-done(((f32[1024,1024]{1,0:T(8,128)}), f32[1024,1024]{1,0:T(8,128)}) %all-reduce.9.cloned.1.call-update) | async-done | bytes 4194320 | tf_op jit(solution)/shard_map/psum | solution.py:91
  109.1 7.2 fusion.95
  116.3 6.7 fusion.94
  123.0 16.6 %multiply_convert_fusion.1 = (bf16[1024,2048]{1,0:T(8,128)(2,1)}, bf16[1024,2048]{1,0:T(8,128)(2,1)}, bf16[1024,2048]{1,0:T(8,128)(2,1)}) fusion(f32[1024,2048]{1,0:T(8,128)} %fusion.94, f32[1024,2048]{1,0:T(8,128)} %fusion.95, bf16[2048,1024]{1,0:T(8,128)(2,1)} %param.28, bf16[1024,1024]{1,0:T(8,128)(2,1)} %all-gather.5.cloned.1.call-done, ...), kind=kOutput, calls=%fused_computation.76 | convolution fusion | flops 4329570304 | bytes 35655680 | tf_op jit(solution)/shard_map/dot_general | solution.py:85
  139.7 6.7 fusion.97
  146.4 6.1 convolution_add_fusion
  152.6 29.7 %all-reduce.11.cloned.1.call-done = f32[1024,1024]{1,0:T(8,128)} async-done(((f32[1024,1024]{1,0:T(8,128)}), f32[1024,1024]{1,0:T(8,128)}) %all-reduce.11.cloned.1.call-update) | async-done | bytes 4194320 | tf_op jit(solution)/shard_map/psum | solution.py:95
  203.2 89.1 %while.33 = (s32[]{:T(128)}, f32[1,1152,8,64]{1,3,2,0:T(8,128)}, f32[1,1152,8,64]{1,3,2,0:T(8,128)}, f32[2,512,8,64]{1,0,3,2:T(2,128)}, s32[2]{0:T(128)S(1)}, /*...) while((s32[]{:T(128)}, f32[1,1152,8,64]{1,3,2,0:T(8,128)}, ...), condition=%wide.region_17.18_spmd.clone, body=%wide.region_15.17_spmd.clone.sunk | while | flops 1720250368 | bytes 103544808 | solution.py:207
  228.2 19.5 %dynamic_update_slice.52 = f32[2,512,8,64]{1,0,3,2:T(2,128)} dynamic-update-slice(f32[2,512,8,64]{1,0,3,2:T(2,128)} %get-tuple-element.653, f32[1,512,8,64]{1,0,3,2:T(1,128)S(1)} %copy.51, s32[]{:T(128)S(6)} %copy.72, s32[]{:T(128)} %constant.208.clone.1..sunk.1, s32[]{:T(128)} %constant.208.clone.1..sunk.1, s32[]{:T(128)} %constant.208.clone.1..sunk.1) | dynamic-update-slice | bytes 2097156 | tf_op jit(solution)/shard_map/while/body/jit(dynamic_update_index_in_dim)/dynamic_update_slice | solution.py:164
  272.6 19.5 %dynamic_update_slice.52 = f32[2,512,8,64]{1,0,3,2:T(2,128)} dynamic-update-slice(f32[2,512,8,64]{1,0,3,2:T(2,128)} %get-tuple-element.653, f32[1,512,8,64]{1,0,3,2:T(1,128)S(1)} %copy.51, s32[]{:T(128)S(6)} %copy.72, s32[]{:T(128)} %constant.208.clone.1..sunk.1, s32[]{:T(128)} %constant.208.clone.1..sunk.1, s32[]{:T(128)} %constant.208.clone.1..sunk.1) | dynamic-update-slice | bytes 2097156 | tf_op jit(solution)/shard_map/while/body/jit(dynamic_update_index_in_dim)/dynamic_update_slice | solution.py:164
  313.3 8.3 convolution_convert_fusion.1
  321.7 8.3 convolution_convert_fusion.2
  331.6 8.8 convolution_convert_fusion
  340.5 10.0 %fusion.96 = f32[1024,1024]{1,0:T(8,128)} fusion(bf16[1024,2048]{1,0:T(8,128)(2,1)} %get-tuple-element.426, bf16[2048,1024]{1,0:T(8,128)(2,1)} %param.28), kind=kOutput, calls=%fused_computation.173 | convolution fusion | flops 4294967296 | bytes 12582912 | tf_op jit(solution)/shard_map/dot_general | solution.py:290
  364.8 12.6 %reduce-scatter.12.cloned.1.call-done = bf16[64,512]{1,0:T(8,128)(2,1)} async-done(((bf16[1024,512]{1,0:T(8,128)(2,1)}), bf16[64,512]{1,0:T(8,128)(2,1)}) %reduce-scatter.12.cloned.1.call-update) | async-done | bytes 65552 | tf_op jit(solution)/shard_map/reduce_scatter | solution.py:347
  378.9 75.0 %reduce-scatter.10.cloned.1.call-done = bf16[64,512]{1,0:T(8,128)(2,1)} async-done(((bf16[1024,512]{1,0:T(8,128)(2,1)}), bf16[64,512]{1,0:T(8,128)(2,1)}) %reduce-scatter.10.cloned.1.call-update) | async-done | bytes 65552 | tf_op jit(solution)/shard_map/reduce_scatter | solution.py:341
  455.4 75.0 %reduce-scatter.8.cloned.1.call-done = bf16[64,512]{1,0:T(8,128)(2,1)} async-done(((bf16[1024,512]{1,0:T(8,128)(2,1)}), bf16[64,512]{1,0:T(8,128)(2,1)}) %reduce-scatter.8.cloned.1.call-update) | async-done | bytes 65552 | tf_op jit(solution)/shard_map/reduce_scatter | solution.py:335
  531.9 92.4 %reduce-scatter.18.cloned.1.call-done = bf16[64,2048]{1,0:T(8,128)(2,1)} async-done(((bf16[1024,2048]{1,0:T(8,128)(2,1)}), bf16[64,2048]{1,0:T(8,128)(2,1)}) %reduce-scatter.18.cloned.1.call-update) | async-done | bytes 262160 | tf_op jit(solution)/shard_map/reduce_scatter | solution.py:307
  626.1 95.1 %reduce-scatter.16.cloned.1.call-done = bf16[64,2048]{1,0:T(8,128)(2,1)} async-done(((bf16[1024,2048]{1,0:T(8,128)(2,1)}), bf16[64,2048]{1,0:T(8,128)(2,1)}) %reduce-scatter.16.cloned.1.call-update) | async-done | bytes 262160 | tf_op jit(solution)/shard_map/reduce_scatter | solution.py:301
  723.0 95.3 %reduce-scatter.20.cloned.1.call-done = bf16[2048,64]{0,1:T(8,128)(2,1)} async-done(((bf16[2048,1024]{0,1:T(8,128)(2,1)}), bf16[2048,64]{0,1:T(8,128)(2,1)}) %reduce-scatter.20.cloned.1.call-update) | async-done | bytes 262160 | tf_op jit(solution)/shard_map/reduce_scatter | solution.py:313
  820.0 39.2 %all-reduce.13.cloned.1.call-done = (f32[1024,1024]{1,0:T(8,128)}, f32[1024,1024]{1,0:T(8,128)}) async-done(((f32[1024,1024]{1,0:T(8,128)}, f32[1024,1024]{1,0:T(8,128)}), (f32[1024,1024]{1,0:T(8,128)}, f32[1024,1024]{1,0:T(8,128)})) %all-reduce.13.cloned.1.call-update) | async-done | bytes 8388624 | tf_op jit(solution)/shard_map/psum | solution.py:91
  871.5 41.2 %all-reduce.3 = (f32[1024]{0:T(1024)}, f32[1024]{0:T(1024)}, f32[1024]{0:T(1024)}, f32[1024]{0:T(1024)}, f32[1024]{0:T(1024)}, /*index=5*/f32[1024]{0:T(1024)}) all-reduce(f32[1024]{0:T(1024)S(1)} %get-tuple-element.431, f32[1024]{0:T(1024)S(1)} %get-tuple-element.432, ...), channel_id=1, replica_groups=mesh['wide'=16,'narrow'=2] {'wide','narrow'}, use_global_device_ids=true, to_apply=%region_29.30 | all-reduce | flops 6144 | bytes 49152 | tf_op jit(solution)/shard_map/psum | solution.py:366
  (267 shorter events, 179.2 us)
Async XLA Ops:
  7.2 59.6 %copy-start = (bf16[512,1024]{1,0:T(8,128)(2,1)S(1)}, bf16[512,1024]{1,0:T(8,128)(2,1)}, u32[]{:S(2)}) copy-start(bf16[512,1024]{1,0:T(8,128)(2,1)} %param.25) | copy-start | bytes 3145732
  7.2 20.1 %copy-start.43 = (f32[1024]{0:T(1024)S(1)}, f32[1024]{0:T(1024)}, u32[]{:S(2)}) copy-start(f32[1024]{0:T(1024)} %param.29) | copy-start | bytes 12292
  7.2 20.1 %copy-start.46 = (f32[1024]{0:T(1024)S(1)}, f32[1024]{0:T(1024)}, u32[]{:S(2)}) copy-start(f32[1024]{0:T(1024)} %param.30) | copy-start | bytes 12292
  7.2 15.7 %all-gather.3.cloned.1.call-start = ((), (), s32[]{:S(2)}) async-start(), calls=%async_computation.7 | async-start | bytes 3145728 | tf_op jit(solution)/shard_map/all_gather | solution.py:240
  8.0 91.8 %all-reduce.9.cloned.1.call-start = ((), (), s32[]{:S(2)}) async-start(), calls=%async_computation.8 | async-start | bytes 8388608 | tf_op jit(solution)/shard_map/psum | solution.py:91
  11.0 25.6 %copy-start.25 = (f32[1024,32]{0,1:T(8,128)}, f32[1024,32]{0,1:T(8,128)S(1)}, u32[]{:S(2)}) copy-start(f32[1024,32]{0,1:T(8,128)S(1)} %get-tuple-element.447) | copy-start | bytes 393220
  11.1 25.6 %copy-start.27 = (f32[1024,32]{0,1:T(8,128)}, f32[1024,32]{0,1:T(8,128)S(1)}, u32[]{:S(2)}) copy-start(f32[1024,32]{0,1:T(8,128)S(1)} %get-tuple-element.448) | copy-start | bytes 393220
  70.0 29.8 %copy-start.47 = (f32[1024]{0:T(1024)S(1)}, f32[1024]{0:T(1024)}, u32[]{:S(2)}) copy-start(f32[1024]{0:T(1024)} %param.33) | copy-start | bytes 12292
  70.0 53.0 %all-gather.5.cloned.1.call-start = ((), (), s32[]{:S(2)}) async-start(), calls=%async_computation.9 | async-start | bytes 3145728 | tf_op jit(solution)/shard_map/all_gather | solution.py:241
  70.8 111.6 %all-reduce.11.cloned.1.call-start = ((), (), s32[]{:S(2)}) async-start(), calls=%async_computation.10 | async-start | bytes 8388608 | tf_op jit(solution)/shard_map/psum | solution.py:95
  123.0 16.7 %copy-start.51 = (bf16[1024,2048]{1,0:T(8,128)(2,1)S(1)}, bf16[1024,2048]{1,0:T(8,128)(2,1)}, u32[]{:S(2)}) copy-start(bf16[1024,2048]{1,0:T(8,128)(2,1)} %param.26) | copy-start | bytes 12582916
  152.6 210.7 %reduce-scatter.14.cloned.1.call-start = ((), (), s32[]{:S(2)}) async-start(), calls=%async_computation.14 | async-start | bytes 1114112 | tf_op jit(solution)/shard_map/reduce_scatter | solution.py:353
  199.9 177.5 %reduce-scatter.12.cloned.1.call-start = ((), (), s32[]{:S(2)}) async-start(), calls=%async_computation.13 | async-start | bytes 1114112 | tf_op jit(solution)/shard_map/reduce_scatter | solution.py:347
  298.4 155.5 %reduce-scatter.10.cloned.1.call-start = ((), (), s32[]{:S(2)}) async-start(), calls=%async_computation.12 | async-start | bytes 1114112 | tf_op jit(solution)/shard_map/reduce_scatter | solution.py:341
  308.0 222.4 %reduce-scatter.8.cloned.1.call-start = ((), (), s32[]{:S(2)}) async-start(), calls=%async_computation.11 | async-start | bytes 1114112 | tf_op jit(solution)/shard_map/reduce_scatter | solution.py:335
  313.2 311.1 %reduce-scatter.18.cloned.1.call-start = ((), (), s32[]{:S(2)}) async-start(), calls=%async_computation.16 | async-start | bytes 4456448 | tf_op jit(solution)/shard_map/reduce_scatter | solution.py:307
  321.6 399.6 %reduce-scatter.16.cloned.1.call-start = ((), (), s32[]{:S(2)}) async-start(), calls=%async_computation.15 | async-start | bytes 4456448 | tf_op jit(solution)/shard_map/reduce_scatter | solution.py:301
  330.0 488.2 %reduce-scatter.20.cloned.1.call-start = ((), (), s32[]{:S(2)}) async-start(), calls=%async_computation.17 | async-start | bytes 4456448 | tf_op jit(solution)/shard_map/reduce_scatter | solution.py:313
  340.4 518.8 %all-reduce.13.cloned.1.call-start = ((), (), s32[]{:S(2)}) async-start(), calls=%async_computation.18 | async-start | bytes 16777216 | tf_op jit(solution)/shard_map/psum | solution.py:91
  340.5 10.1 %copy-start.36 = (bf16[1024,8,64]{0,2,1:T(8,128)(2,1)S(1)}, bf16[1024,8,64]{0,2,1:T(8,128)(2,1)}, u32[]{:S(2)}) copy-start(bf16[1024,8,64]{0,2,1:T(8,128)(2,1)} %copy-done.35) | copy-start | bytes 3145732
  361.1 498.1 %copy-start.3 = (bf16[1024,1024]{1,0:T(8,128)(2,1)S(1)}, bf16[1024,1024]{1,0:T(8,128)(2,1)}, u32[]{:S(2)}) copy-start(bf16[1024,1024]{1,0:T(8,128)(2,1)} %all-gather.3.cloned.1.call-done) | copy-start | bytes 6291460
  361.1 498.1 %copy-start.39 = (f32[1024]{0:T(1024)S(1)}, f32[1024]{0:T(1024)}, u32[]{:S(2)}) copy-start(f32[1024]{0:T(1024)} %copy-done.38) | copy-start | bytes 12292
  361.1 498.1 %copy-start.44 = (f32[1024]{0:T(1024)S(1)}, f32[1024]{0:T(1024)}, u32[]{:S(2)}) copy-start(f32[1024]{0:T(1024)} %param.29) | copy-start | bytes 12292
  867.9 44.8 %copy-start.1 = (bf16[512,1024]{1,0:T(8,128)(2,1)S(1)}, bf16[512,1024]{1,0:T(8,128)(2,1)}, u32[]{:S(2)}) copy-start(bf16[512,1024]{1,0:T(8,128)(2,1)} %param.25) | copy-start | bytes 3145732
  (52 other events, 188.2 us)
Sparse Core Ops, SparseCore 0:
  9.6 13.2 all-gather.2
  70.1 29.5 all-reduce.8
  101.4 11.7 all-gather.4
  152.7 29.6 all-reduce.10
  200.0 78.9 reduce-scatter.13
  298.5 78.8 reduce-scatter.11
  379.7 74.1 reduce-scatter.9
  456.2 74.0 reduce-scatter.7
  532.7 91.6 reduce-scatter.17
  626.5 94.7 reduce-scatter.15
  723.5 94.6 reduce-scatter.19
  820.7 38.5 all-reduce.12
where the time goes:
time: 930 us; the launch traced here: 920 us
  waiting for transfers between devices  557 us (60%)
  matrix products  154 us (17%)
  local copies, waits for them, and re-layouts  74.3 us (8%)
  other arithmetic  67 us (7%)
  blocking collectives  41.2 us (4%)
  between operations  15.1 us (2%)
  loops' own time  11.3 us (1%)
    reduce_scatter x1, waiting for transfers between devices, on_device(): lax.psum_scatter(down_part.astype(jnp.bfloat16), 'wide', scatter_dimensio...  95.3 us
    reduce_scatter x1, waiting for transfers between devices, on_device(): lax.psum_scatter(row_contract(mlp_in, gate_back).astype(jnp.bfloat16), 'w...  95.1 us
    reduce_scatter x1, waiting for transfers between devices, on_device(): lax.psum_scatter(row_contract(mlp_in, up_back).astype(jnp.bfloat16), 'wid...  92.4 us
    reduce_scatter x1, waiting for transfers between devices, on_device(): lax.psum_scatter(row_contract(attn_in, key_pre_grad).astype(jnp.bfloat16)...  75 us
    reduce_scatter x1, waiting for transfers between devices, on_device(): lax.psum_scatter(row_contract(attn_in, query_pre_grad).astype(jnp.bfloat1...  75 us
    psum x2, waiting for transfers between devices, reduce_forward(): return lax.psum(partial_sum, 'narrow')  68.1 us
    psum x1, blocking collectives, on_device(): lax.psum((jnp.sum(own_one_grad * own_rows(unit_one), axis=0), jnp.sum(own...  41.2 us
    dynamic_update_slice x4, local copies, waits for them, and re-layouts, attention_forward(): return lax.map(forward_block, jnp.arange(total_blocks, dtype=jnp.int32))  41.2 us
  transfers between devices with their start and end apart: 12, of which 10 were waited for; matrix products, arithmetic and copies ran while one was open for 20% of the time, Pallas kernels for 0%

commit v1 on v0

v1 whole, which is shorter than its diff:
```python
import functools
import math

import jax
import jax.numpy as jnp
import numpy as np
from jax import lax
from jax.experimental import pallas as pl
from jax.experimental.pallas import tpu as pltpu
from jax.sharding import PartitionSpec as P

HEAD_DIM = 64
HALF_WINDOW = 64
CLIPS = 6
MAX_CLIP = 384
norm_eps = 1e-05
masked_score = -1e30
bf16 = jnp.bfloat16
f32 = jnp.float32
NN = (((1,), (0,)), ((), ()))
NT = (((1,), (1,)), ((), ()))
TN = (((0,), (0,)), ((), ()))


def dot(a, b, dims=NN):
    return lax.dot_general(a, b, dims, preferred_element_type=f32)


def call(body, name, grid, in_specs, out_specs, out_shape, scratch=(), prefetch=0, mib=48):
    return pl.pallas_call(
        body,
        grid_spec=pltpu.PrefetchScalarGridSpec(
            num_scalar_prefetch=prefetch,
            grid=grid,
            in_specs=in_specs,
            out_specs=out_specs,
            scratch_shapes=list(scratch),
        ),
        out_shape=out_shape,
        compiler_params=pltpu.CompilerParams(vmem_limit_bytes=mib * 2**20),
        name=name,
    )


def whole(shape):
    return pl.BlockSpec(
        shape, lambda *_: (0,) * len(shape), pipeline_mode=pl.Buffered(1)
    )


def like(shape, kind=bf16):
    return jax.ShapeDtypeStruct(shape, kind)


def normalise(rows):
    centred = rows - jnp.mean(rows, axis=-1, keepdims=True)
    inverse = lax.rsqrt(jnp.mean(centred * centred, axis=-1, keepdims=True) + norm_eps)
    return centred * inverse, inverse


def norm_back(incoming, unit, inverse, gain):
    scaled = incoming * gain
    return inverse * (
        scaled
        - jnp.mean(scaled, axis=-1, keepdims=True)
        - unit * jnp.mean(scaled * unit, axis=-1, keepdims=True)
    )


def rope_table():
    half = HEAD_DIM // 2
    lane = np.arange(128)
    frequency = np.exp((lane % half) * (-math.log(10000.0) / half))
    angle = np.arange(MAX_CLIP)[:, None] * frequency[None, :]
    sign = np.where(lane % HEAD_DIM < half, -1.0, 1.0)
    parts = []
    for table in (np.cos(angle), np.sin(angle) * sign):
        high = table.astype(np.float32).astype(bf16)
        parts += [high, (table - high.astype(np.float64)).astype(np.float32).astype(bf16)]
    return np.concatenate(parts, axis=1)


def swap_halves(values):
    half = HEAD_DIM // 2
    width = values.shape[-1]
    lane = lax.broadcasted_iota(jnp.int32, values.shape, 1)
    return jnp.where(
        lane % HEAD_DIM < half,
        pltpu.roll(values, width - half, 1),
        pltpu.roll(values, half, 1),
    )


def column_of(row, start, count):
    pieces = []
    for place in range(count // 128):
        piece = row[:, pl.ds(pl.multiple_of(start + place * 128, 128), 128)]
        pieces.append(jnp.broadcast_to(piece.astype(f32), (128, 128)).T)
    return jnp.concatenate(pieces, axis=0) if len(pieces) > 1 else pieces[0]


def project_body(core, own, other, seg, gain, bias, table, wq, wk, wv, q, k, v, u, x, cos, sin, *, own_blocks, blocks):
    step = pl.program_id(0)
    block = lax.rem(step + core[0] * own_blocks, blocks)
    rows_per = own.shape[0]
    raw = jnp.where(step < own_blocks, own[...], other[...])
    x[...] = raw
    unit, _ = normalise(raw.astype(f32))
    normed = (unit * gain[...] + bias[...]).astype(bf16)
    u[...] = normed
    ids = seg[...]
    mine = column_of(seg, block * rows_per, rows_per)
    start = jnp.zeros_like(mine)
    for clip in range(CLIPS - 1):
        count = jnp.sum((ids == clip).astype(f32), axis=-1, keepdims=True)
        start += jnp.where(mine > clip, count, 0.0)
    place = lax.broadcasted_iota(jnp.int32, mine.shape, 0) + block * rows_per
    place = place - start.astype(jnp.int32)
    lane = lax.broadcasted_iota(jnp.int32, mine.shape, 1)
    hot = jnp.concatenate(
        [(place == lane + 128 * part).astype(bf16) for part in range(MAX_CLIP // 128)], axis=1
    )
    rows = dot(hot, table[...])
    cosine = rows[:, :128] + rows[:, 128:256]
    sine = rows[:, 256:384] + rows[:, 384:]
    cos[...] = cosine
    sin[...] = sine

    def turned(weights):
        flat = dot(normed, weights)
        return [
            flat[:, at : at + 128] * cosine + swap_halves(flat[:, at : at + 128]) * sine
            for at in range(0, flat.shape[1], 128)
        ]

    for pair, values in enumerate(turned(wq[...])):
        q[:, pair * 128 : pair * 128 + 128] = (values * HEAD_DIM**-0.5).astype(bf16)
    for pair, values in enumerate(turned(wk[...])):
        k[:, pair * 128 : pair * 128 + 128] = values.astype(bf16)
    v[...] = dot(normed, wv[...]).astype(bf16)


def project(core, pieces, seg, gain, bias, wq, wk, wv, rows_per=256):
    own, other = pieces if len(pieces) == 2 else (pieces[0], pieces[0])
    own_blocks = own.shape[0] // rows_per
    length, width = own.shape[0] * len(pieces), own.shape[1]
    blocks = length // rows_per
    heads = wq.shape[1]

    def out(columns):
        return pl.BlockSpec(
            (rows_per, columns), lambda i, core: (lax.rem(i + core[0] * own_blocks, blocks), 0)
        )

    table = rope_table()
    return call(
        functools.partial(project_body, own_blocks=own_blocks, blocks=blocks),
        "project",
        (blocks,),
        [
            pl.BlockSpec((rows_per, width), lambda i, core: (jnp.minimum(i, own_blocks - 1), 0)),
            pl.BlockSpec(
                (rows_per, width),
                lambda i, core: (jnp.maximum(i - own_blocks, 0) if len(pieces) == 2 else 0, 0),
            ),
            whole(seg.shape),
            whole((1, width)),
            whole((1, width)),
            whole(table.shape),
            whole(wq.shape),
            whole(wk.shape),
            whole(wv.shape),
        ],
        [out(heads)] * 3 + [out(width)] * 2 + [out(128)] * 2,
        [like((length, heads))] * 3 + [like((length, width))] * 2 + [like((length, 128), f32)] * 2,
        prefetch=1,
    )(core, own, other, seg, gain, bias, jnp.asarray(table), wq, wk, wv)


def band(seg, block, rows_per, span, length):
    first = block * rows_per
    start = jnp.clip(first - HALF_WINDOW, 0, length - span)
    return first, pl.multiple_of(start, HALF_WINDOW)


def two_heads(values):
    lane = lax.broadcasted_iota(jnp.int32, values.shape, 1)
    zero = jnp.zeros_like(values)
    return jnp.concatenate(
        [jnp.where(lane < HEAD_DIM, values, zero), jnp.where(lane < HEAD_DIM, zero, values)], axis=0
    )


def one_each(stacked):
    count = stacked.shape[0] // 2
    lane = lax.broadcasted_iota(jnp.int32, (count, 128), 1)
    return jnp.where(lane < HEAD_DIM, stacked[:count], stacked[count:])


def attend_body(q, k, v, seg, segw, o, weights, *, offset, span):
    rows_per = q.shape[0]
    length = k.shape[0]
    block = pl.program_id(0) + offset
    first, start = band(seg, block, rows_per, span, length)
    mine = column_of(seg, first, rows_per)
    theirs = segw[pl.ds(lax.div(start, HALF_WINDOW), 1), :]
    gap = (
        lax.broadcasted_iota(jnp.int32, (rows_per, span), 1)
        - lax.broadcasted_iota(jnp.int32, (rows_per, span), 0)
        + (start - first)
    )
    mine_wide = jnp.concatenate([mine] * (span // 128), axis=1)
    allowed = (gap >= -HALF_WINDOW) & (gap < HALF_WINDOW) & (mine_wide == theirs.astype(f32))
    penalty = jnp.where(allowed, 0.0, masked_score)
    penalty = jnp.concatenate([penalty, penalty], axis=0)
    for pair in range(q.shape[1] // 128):
        lanes = slice(pair * 128, pair * 128 + 128)
        keys = k[pl.ds(start, span), lanes]
        values = v[pl.ds(start, span), lanes]
        scores = dot(two_heads(q[:, lanes]), keys, NT) + penalty
        lifted = jnp.exp(scores - jnp.max(scores, axis=-1, keepdims=True))
        chances = (lifted * (1.0 / jnp.sum(lifted, axis=-1, keepdims=True))).astype(bf16)
        weights[0, pair] = chances
        o[:, lanes] = one_each(dot(chances, values)).astype(bf16)


def windows(seg, span):
    length = seg.shape[1]
    return jnp.concatenate(
        [
            seg[:, min(at, length - span) : min(at, length - span) + span]
            for at in range(0, length, HALF_WINDOW)
        ],
        axis=0,
    )


def attend(q, k, v, seg, segw, offset, blocks, rows_per, span):
    length, heads = q.shape
    pairs = heads // 128
    return call(
        functools.partial(attend_body, offset=offset, span=span),
        "attend",
        (blocks,),
        [
            pl.BlockSpec((rows_per, heads), lambda i: (i + offset, 0)),
            whole(k.shape),
            whole(v.shape),
            whole(seg.shape),
            whole(segw.shape),
        ],
        [
            pl.BlockSpec((rows_per, heads), lambda i: (i, 0)),
            pl.BlockSpec((1, pairs, 2 * rows_per, span), lambda i: (i, 0, 0, 0)),
        ],
        [like((blocks * rows_per, heads)), like((blocks, pairs, 2 * rows_per, span))],
    )(q, k, v, seg, segw)


def attend_back_body(go, q, k, v, wa, wb, cos, sin, gq, gk, gv, acc_k, acc_v, *, span, half_blocks):
    rows_per = q.shape[0]
    length = k.shape[0]
    block = pl.program_id(0)
    _, start = band(None, block, rows_per, span, length)

    @pl.when(block == 0)
    def _():
        acc_k[...] = jnp.zeros_like(acc_k)
        acc_v[...] = jnp.zeros_like(acc_v)

    mine = pl.ds(pl.multiple_of(block * rows_per, rows_per), rows_per)
    cosine, sine = cos[mine, :], sin[mine, :]
    keys_at = pl.ds(start, span)
    for pair in range(q.shape[1] // 128):
        lanes = slice(pair * 128, pair * 128 + 128)
        keys = k[keys_at, lanes]
        values = v[keys_at, lanes]
        chances = jnp.where(block < half_blocks, wa[0, pair], wb[0, pair])
        full = chances.astype(f32)
        go_two = two_heads(go[:, lanes])
        change = dot(go_two, values, NT)
        weighted = jnp.sum(full * change, axis=-1, keepdims=True)
        gs = (full * (change - weighted)).astype(bf16)
        gq_rows = one_each(dot(gs, keys)) * HEAD_DIM**-0.5
        gq[:, lanes] = (gq_rows * cosine - swap_halves(gq_rows) * sine).astype(bf16)
        acc_k[keys_at, lanes] += dot(gs, two_heads(q[:, lanes]), TN)
        acc_v[keys_at, lanes] += dot(chances, go_two, TN)

    @pl.when(block == pl.num_programs(0) - 1)
    def _():
        gv[...] = acc_v[...].astype(bf16)
        for pair in range(q.shape[1] // 128):
            lanes = slice(pair * 128, pair * 128 + 128)
            rows = acc_k[:, lanes]
            gk[:, lanes] = (rows * cos[...] - swap_halves(rows) * sin[...]).astype(bf16)


def attend_back(go, q, k, v, wa, wb, cos, sin, rows_per, span):
    length, heads = q.shape
    pairs = heads // 128
    blocks = length // rows_per
    half = blocks // 2
    row = pl.BlockSpec((rows_per, heads), lambda i: (i, 0))
    chance = (1, pairs, 2 * rows_per, span)
    return call(
        functools.partial(attend_back_body, span=span, half_blocks=half),
        "attend_back",
        (blocks,),
        [
            row,
            row,
            whole(k.shape),
            whole(v.shape),
            pl.BlockSpec(chance, lambda i: (jnp.minimum(i, half - 1), 0, 0, 0)),
            pl.BlockSpec(chance, lambda i: (jnp.maximum(i - half, 0), 0, 0, 0)),
            whole(cos.shape),
            whole(sin.shape),
        ],
        [row, whole(k.shape), whole(k.shape)],
        [like((length, heads))] * 3,
        scratch=[pltpu.VMEM((length, heads), f32)] * 2,
    )(go, q, k, v, wa, wb, cos, sin)


def put_transposed(target, places, values, at, piece):
    for group in range(values.shape[1] // 128):
        turned = values[:, group * 128 : group * 128 + 128].T
        for part in range(128 // piece):
            place = places[group * (128 // piece) + part]
            target[pl.ds(pl.multiple_of(place * piece, piece), piece), at] = turned[
                part * piece : part * piece + piece
            ]


def cotangent_body(core, places, own, other, scale, dy, gm, gmt, *, own_blocks, blocks, piece):
    step = pl.program_id(0)
    raw = jnp.where(step < own_blocks, own[...], other[...])
    dy[...] = raw
    scaled = (raw.astype(f32) * scale[...]).astype(bf16)
    gm[...] = scaled
    put_transposed(gmt, places, scaled, slice(None), piece)


def cotangent(core, places, pieces, scale, piece, rows_per=256):
    own, other = pieces if len(pieces) == 2 else (pieces[0], pieces[0])
    own_blocks = own.shape[0] // rows_per
    length, width = own.shape[0] * len(pieces), own.shape[1]
    blocks = length // rows_per

    def at(i, core):
        return lax.rem(i + core[0] * own_blocks, blocks)

    row = pl.BlockSpec((rows_per, width), lambda i, core, places: (at(i, core), 0))
    return call(
        functools.partial(cotangent_body, own_blocks=own_blocks, blocks=blocks, piece=piece),
        "cotangent",
        (blocks,),
        [
            pl.BlockSpec(
                (rows_per, width), lambda i, core, places: (jnp.minimum(i, own_blocks - 1), 0)
            ),
            pl.BlockSpec(
                (rows_per, width),
                lambda i, core, places: (
                    jnp.maximum(i - own_blocks, 0) if len(pieces) == 2 else 0,
                    0,
                ),
            ),
            whole((1, width)),
        ],
        [row, row, pl.BlockSpec((width, rows_per), lambda i, core, places: (0, at(i, core)))],
        [like((length, width)), like((length, width)), like((width, length))],
        prefetch=2,
    )(core, places, own, other, scale)


def turn_body(places, values, out, *, piece):
    put_transposed(out, places, values[...], slice(None), piece)


def turn(places, values, piece, rows_per=256):
    length, width = values.shape
    return call(
        functools.partial(turn_body, piece=piece),
        "turn",
        (length // rows_per,),
        [pl.BlockSpec((rows_per, width), lambda i, places: (i, 0))],
        [pl.BlockSpec((width, rows_per), lambda i, places: (0, i))],
        [like((width, length))],
        prefetch=1,
    )(places, values)[0]


def middle_body(places, *refs, parts, piece):
    mixed = refs[: 2 * parts]
    x, scale, gain, bias, attn, m, mt = refs[2 * parts :]
    total = dot(mixed[0][...], mixed[1][...])
    for part in range(1, parts):
        total += dot(mixed[2 * part][...], mixed[2 * part + 1][...])
    low = total.astype(bf16)
    attn[...] = low
    middle = x[...].astype(f32) + scale[...] * low.astype(f32)
    unit, _ = normalise(middle)
    normed = (unit * gain[...] + bias[...]).astype(bf16)
    m[...] = normed
    put_transposed(mt, places, normed, slice(None), piece)


def middle(places, mixed, x, offset, scale, gain, bias, piece, rows_per=256):
    rows, width = mixed[0][0].shape[0], x.shape[1]
    blocks = rows // rows_per
    specs, operands = [], []
    for left, right in mixed:
        specs += [
            pl.BlockSpec((rows_per, left.shape[1]), lambda i, places: (i, 0)),
            whole(right.shape),
        ]
        operands += [left, right]
    row = pl.BlockSpec((rows_per, width), lambda i, places: (i, 0))
    return call(
        functools.partial(middle_body, parts=len(mixed), piece=piece),
        "middle",
        (blocks,),
        specs
        + [
            pl.BlockSpec((rows_per, width), lambda i, places: (i + offset // rows_per, 0)),
            whole((1, width)),
            whole((1, width)),
            whole((1, width)),
        ],
        [row, row, pl.BlockSpec((width, rows_per), lambda i, places: (0, i))],
        [like((rows, width)), like((rows, width)), like((width, rows))],
        prefetch=1,
    )(places, *operands, x, scale, gain, bias)


def sent_shapes(fast, rows, first, second):
    if fast:
        half = rows // 2
        return [(half, first), (half, first), (half, second), (half, second)]
    return [(rows, first + second)]


def put_rows(outs, fast, quarter, height, left, right):
    if not fast:
        at = slice(quarter * height, quarter * height + height)
        outs[0][at, :] = jnp.concatenate([left, right], axis=1)
        return
    send_a, keep_a, send_b, keep_b = outs
    place = slice((quarter % 2) * height, (quarter % 2) * height + height)
    (send_a if quarter < 2 else keep_a)[place, :] = left
    place = slice((quarter // 2) * height, (quarter // 2) * height + height)
    (send_b if quarter % 2 == 0 else keep_b)[place, :] = right


def feed_body(ma, mb, gm, mta, mtb, gmt, wg, wu, wd, hid, gg, gu, *outs, fast, rows_per):
    half = ma.shape[0]
    for source, base in ((ma, 0), (mb, half)):
        for at in range(0, half, rows_per):
            here = slice(at, at + rows_per)
            there = slice(base + at, base + at + rows_per)
            rows = source[here, :]
            gate = dot(rows, wg[...])
            up = dot(rows, wu[...])
            back = dot(gm[there, :], wd[...], NT)
            sigma = 1.0 / (1.0 + jnp.exp(-gate))
            active = gate * sigma
            hid[there, :] = (active * up).astype(bf16)
            gg[there, :] = (back * up * sigma * (1.0 + gate * (1.0 - sigma))).astype(bf16)
            gu[there, :] = (back * active).astype(bf16)
    width = gmt.shape[0]
    height = width // 4
    columns = hid.shape[1]
    for quarter in range(4):
        rows = slice(quarter * height, quarter * height + height)
        down = dot(gmt[rows, :], hid[...]).astype(bf16)
        left, right = mta[rows, :], mtb[rows, :]
        gate = (dot(left, gg[:half, :]) + dot(right, gg[half:, :])).astype(bf16)
        up = (dot(left, gu[:half, :]) + dot(right, gu[half:, :])).astype(bf16)
        put_rows(
            outs,
            fast,
            quarter,
            height,
            jnp.concatenate([down, gate[:, : columns // 2]], axis=1),
            jnp.concatenate([gate[:, columns // 2 :], up], axis=1),
        )


def feed(fast, m, gm, mt, gmt, wg, wu, wd, first, count, columns, rows_per=256):
    length, width = gm.shape
    half = m[0].shape[0]
    col = pl.BlockSpec((width, columns), lambda j: (0, j + first))
    out = pl.BlockSpec((length, columns), lambda j: (0, j))
    part = columns + columns // 2
    shapes = sent_shapes(fast, width, part, part)
    return call(
        functools.partial(feed_body, fast=fast, rows_per=min(rows_per, half)),
        "feed",
        (count,),
        [whole((half, width))] * 2
        + [whole((length, width))]
        + [whole((width, half))] * 2
        + [whole((width, length))]
        + [col, col, pl.BlockSpec((columns, width), lambda j: (j + first, 0))],
        [out] * 3 + [pl.BlockSpec(shape, lambda j: (0, j)) for shape in shapes],
        [like((length, columns * count))] * 3
        + [like((shape[0], shape[1] * count)) for shape in shapes],
        mib=52,
    )(*m, gm, *mt, gmt, wg, wu, wd)


def split_rows(fast, core, rows, rows_per):
    blocks = rows // rows_per
    own = blocks // 2 if fast else blocks

    def at(i, core):
        return lax.rem(i + (1 - core[0]) * own, blocks) if fast else i

    return blocks, own, at


def multiply_body(core, *refs, parts, dims, own, fast):
    lefts, rights = refs[:parts], refs[parts : 2 * parts]
    total = dot(lefts[0][...], rights[0][...], dims)
    for part in range(1, parts):
        total += dot(lefts[part][...], rights[part][...], dims)
    if fast:
        sent, kept = refs[2 * parts :]

        @pl.when(pl.program_id(0) < own)
        def _():
            sent[...] = total.astype(bf16)

        @pl.when(pl.program_id(0) >= own)
        def _():
            kept[...] = total.astype(bf16)
    else:
        refs[2 * parts][...] = total


def multiply(fast, core, lefts, rights, dims, name, rows_per=256):
    rows = lefts[0].shape[0]
    width = rights[0].shape[1 if dims is NN else 0]
    blocks, own, at = split_rows(fast, core, rows, rows_per)
    left_specs = [
        pl.BlockSpec((rows_per, left.shape[1]), lambda i, core: (at(i, core), 0)) for left in lefts
    ]
    if fast:
        out_specs = [
            pl.BlockSpec((rows_per, width), lambda i, core: (jnp.minimum(i, own - 1), 0)),
            pl.BlockSpec((rows_per, width), lambda i, core: (jnp.maximum(i - own, 0), 0)),
        ]
        out_shape = [like((own * rows_per, width))] * 2
    else:
        out_specs = [pl.BlockSpec((rows_per, width), lambda i, core: (i, 0))]
        out_shape = [like((rows, width), f32)]
    return call(
        functools.partial(multiply_body, parts=len(lefts), dims=dims, own=own, fast=fast),
        name,
        (blocks,),
        left_specs + [whole(right.shape) for right in rights],
        out_specs,
        out_shape,
        prefetch=1,
    )(core, *lefts, *rights)


def middle_back_body(
    core, places, *refs, parts, own_blocks, blocks, piece
):
    partial = refs[:parts]
    x, attn, dy, scale, gain, wo, gh, ga_t, go, sums = refs[parts:]
    step = pl.program_id(0)
    incoming = partial[0][...].astype(f32)
    for part in range(1, parts):
        incoming += partial[part][...].astype(f32)
    attn_rows = attn[...].astype(f32)
    unit, inverse = normalise(x[...].astype(f32) + scale[...] * attn_rows)
    grad = dy[...].astype(f32) + norm_back(incoming, unit, inverse, gain[...])
    gh[...] = grad
    ga = (scale[...] * grad).astype(bf16)
    put_transposed(ga_t, places, ga, slice(None), piece)
    go[...] = dot(ga, wo[...], NT).astype(bf16)

    @pl.when(step == 0)
    def _():
        sums[...] = jnp.zeros_like(sums)

    first = core[0] * own_blocks

    @pl.when((step >= first) & (step < first + own_blocks))
    def _():
        sums[0:1, :] += jnp.sum(incoming * unit, axis=0, keepdims=True)
        sums[1:2, :] += jnp.sum(incoming, axis=0, keepdims=True)
        sums[2:3, :] += jnp.sum(attn_rows * grad, axis=0, keepdims=True)


def middle_back(core, places, partial, x, attn, dy, scale, gain, wo, own_rows, piece, rows_per=256):
    length, width = x.shape
    row = pl.BlockSpec((rows_per, width), lambda i, core, places: (i, 0))
    heads = wo.shape[0]
    half = attn[0].shape[0] // rows_per
    return call(
        functools.partial(
            middle_back_body,
            parts=len(partial),
            own_blocks=own_rows // rows_per if own_rows >= rows_per else 1,
            blocks=length // rows_per,
            piece=piece,
        ),
        "middle_back",
        (length // rows_per,),
        [row] * len(partial) + [row, row, row, whole((1, width)), whole((1, width)), whole(wo.shape)],
        [
            row,
            pl.BlockSpec((width, rows_per), lambda i, core, places: (0, i)),
            pl.BlockSpec((rows_per, heads), lambda i, core, places: (i, 0)),
            whole((8, width)),
        ],
        [
            like((length, width), f32),
            like((width, length)),
            like((length, heads)),
            like((8, width), f32),
        ],
        prefetch=2,
    )(core, places, *partial, x, jnp.concatenate(attn, axis=0), dy, scale, gain, wo)


def weights_body(ut, gat, o, gq, gk, gv, *outs, fast):
    width = ut.shape[0]
    height = width // 4
    for quarter in range(4):
        rows = slice(quarter * height, quarter * height + height)
        left = ut[rows, :]
        put_rows(
            outs,
            fast,
            quarter,
            height,
            jnp.concatenate(
                [dot(left, gq[...]).astype(bf16), dot(gat[rows, :], o[...]).astype(bf16)], axis=1
            ),
            jnp.concatenate(
                [dot(left, gk[...]).astype(bf16), dot(left, gv[...]).astype(bf16)], axis=1
            ),
        )


def attention_weights(fast, ut, gat, o, gq, gk, gv):
    width = ut.shape[0]
    heads = gq.shape[1]
    shapes = sent_shapes(fast, width, 2 * heads, 2 * heads)
    operands = (ut, gat, o, gq, gk, gv)
    return call(
        functools.partial(weights_body, fast=fast),
        "attention_weights",
        (1,),
        [whole(operand.shape) for operand in operands],
        [whole(shape) for shape in shapes],
        [like(shape) for shape in shapes],
    )(*operands)


def output_body(*refs, parts):
    partial = refs[:parts]
    x, attn, dy, scale_attn, scale_mlp, out, sums = refs[parts:]
    total = partial[0][...].astype(f32)
    for part in range(1, parts):
        total += partial[part][...].astype(f32)
    middle_rows = x[...].astype(f32) + scale_attn[...] * attn[...].astype(f32)
    out[...] = (middle_rows + scale_mlp[...] * total).astype(bf16)

    @pl.when(pl.program_id(0) == 0)
    def _():
        sums[...] = jnp.zeros_like(sums)

    sums[3:4, :] += jnp.sum(total * dy[...].astype(f32), axis=0, keepdims=True)


def output_rows(core, partial, x, attn, dy, scale_attn, scale_mlp, rows_per=256):
    rows, width = x.shape
    rows_per = min(rows_per, rows)
    row = pl.BlockSpec((rows_per, width), lambda i: (i, 0))
    return call(
        functools.partial(output_body, parts=len(partial)),
        "output_rows",
        (rows // rows_per,),
        [row] * len(partial) + [row] * 3 + [whole((1, width))] * 2,
        [row, whole((8, width))],
        [like((rows, width)), like((8, width), f32)],
    )(*partial, x, attn, dy, scale_attn, scale_mlp)


def input_body(*refs, parts):
    partial = refs[:parts]
    x, gh, gain, out, sums = refs[parts:]
    incoming = partial[0][...].astype(f32)
    for part in range(1, parts):
        incoming += partial[part][...].astype(f32)
    unit, inverse = normalise(x[...].astype(f32))
    out[...] = (gh[...] + norm_back(incoming, unit, inverse, gain[...])).astype(bf16)

    @pl.when(pl.program_id(0) == 0)
    def _():
        sums[...] = jnp.zeros_like(sums)

    sums[4:5, :] += jnp.sum(incoming * unit, axis=0, keepdims=True)
    sums[5:6, :] += jnp.sum(incoming, axis=0, keepdims=True)


def input_rows(partial, x, gh, gain, rows_per=256):
    rows, width = x.shape
    rows_per = min(rows_per, rows)
    row = pl.BlockSpec((rows_per, width), lambda i: (i, 0))
    return call(
        functools.partial(input_body, parts=len(partial)),
        "input_rows",
        (rows // rows_per,),
        [row] * len(partial) + [row] * 2 + [whole((1, width))],
        [row, whole((8, width))],
        [like((rows, width)), like((8, width), f32)],
    )(*partial, x, gh, gain)


class Wide:
    def __init__(self):
        self.size = lax.axis_size("wide")
        self.fast = self.size == 16
        self.place = lax.axis_index("wide")

    def order(self):
        groups = jnp.arange(self.size, dtype=jnp.int32)
        if not self.fast:
            return groups
        mine = self.place.astype(jnp.int32)
        near = 1 - ((groups ^ mine) & 1)
        far = 1 - (((groups ^ mine) >> 1) & 1)
        line = (groups // 4 - mine // 4) % 4
        return near * 8 + far * 4 + line

    def along(self, values, bit):
        return lax.ppermute(values, "wide", [(i, i ^ bit) for i in range(self.size)])

    def reduce(self, outs):
        if not self.fast:
            return lax.psum_scatter(outs[0], "wide", scatter_dimension=0, tiled=True).astype(f32)
        send_a, keep_a, send_b, keep_b = outs
        part_a = keep_a + self.along(send_a, 1)
        part_b = keep_b + self.along(send_b, 2)
        half = part_a.shape[0] // 2
        part_a = part_a[half:] + self.along(part_a[:half], 2)
        part_b = part_b[half:] + self.along(part_b[:half], 1)
        both = jnp.concatenate([part_a, part_b], axis=1)
        height = both.shape[0] // 4
        total = both[:height].astype(f32)
        for shift in (1, 2, 3):
            moved = lax.ppermute(
                both[shift * height : shift * height + height],
                "wide",
                [(i, (i + 4 * shift) % 16) for i in range(16)],
            )
            total += moved.astype(f32)
        return total


def on_device(
    frames,
    segment_ids,
    w_query,
    w_key,
    w_value,
    w_out,
    w_gate,
    w_up,
    w_down,
    norm1_gain,
    norm1_bias,
    norm2_gain,
    norm2_bias,
    scale_attn,
    scale_mlp,
    output_grad,
):
    paired = lax.axis_size("narrow") == 2
    narrow = lax.axis_index("narrow").astype(jnp.int32)
    core = (narrow if paired else jnp.zeros_like(narrow)).reshape(1)
    wide = Wide()
    places = wide.order()
    rows_own, width = frames.shape
    length = segment_ids.shape[1]
    piece = width // wide.size
    heads = w_query.shape[1]
    units = w_gate.shape[1]
    row = lambda vector: vector.reshape(1, -1)
    gain1, bias1, gain2, bias2 = map(row, (norm1_gain, norm1_bias, norm2_gain, norm2_bias))
    scale1, scale2 = row(scale_attn), row(scale_mlp)

    def swapped(values):
        return lax.ppermute(values, "narrow", [(0, 1), (1, 0)])

    def rows_of_all(values):
        if paired:
            return (values, swapped(values))
        return (lax.all_gather(values, "narrow", axis=0, tiled=True),)

    def own_of(values):
        return lax.dynamic_slice_in_dim(values, narrow * rows_own, rows_own, 0)

    frame_rows = rows_of_all(frames)
    grad_rows = rows_of_all(output_grad)
    q, k, v, u, x, cos, sin = project(
        core, frame_rows, segment_ids, gain1, bias1, w_query, w_key, w_value
    )
    rows_per = 128
    span = rows_per + 2 * HALF_WINDOW
    segw = windows(segment_ids, span)
    half = length // 2
    if paired:
        w_out_all = (w_out, swapped(w_out))
    else:
        w_out_all = (lax.all_gather(w_out, "narrow", axis=0, tiled=True),)
    dy, gm, gmt = cotangent(core, places, grad_rows, scale2, piece)
    mixed, chances, attn, m, mt = [], [], [], [], []
    for part in range(2):
        o_part, p_part = attend(
            q, k, v, segment_ids, segw, part * half // rows_per, half // rows_per, rows_per, span
        )
        mixed.append(o_part)
        chances.append(p_part)
        if paired:
            o_all = (o_part, swapped(o_part))
        else:
            o_all = (lax.all_gather(o_part, "narrow", axis=1, tiled=True),)
        attn_part, m_part, mt_part = middle(
            places, list(zip(o_all, w_out_all)), x, part * half, scale1, gain2, bias2, piece
        )
        attn.append(attn_part)
        m.append(m_part)
        mt.append(mt_part)
    o = jnp.concatenate(mixed, axis=0)

    columns = min(256, units)
    total = units // columns
    counts = [1, 2, 2, 3] if total == 8 else [total]
    hidden, g_gate, g_up, groups = [], [], [], []
    first = 0
    for count in counts:
        hid, gg, gu, *outs = feed(
            wide.fast, m, gm, mt, gmt, w_gate, w_up, w_down, first, count, columns
        )
        hidden.append(hid)
        g_gate.append(gg)
        g_up.append(gu)
        total_rows = wide.reduce(outs)
        if wide.fast:
            total_rows = total_rows.reshape(piece, 2, count, -1).swapaxes(1, 2)
        groups.append(total_rows.reshape(piece, count, 3, columns))
        first += count
    hidden = jnp.concatenate(hidden, axis=1)
    g_gate = jnp.concatenate(g_gate, axis=1)
    g_up = jnp.concatenate(g_up, axis=1)

    def combined(lefts, rights, dims, name, every):
        if paired:
            sent, kept = multiply(True, core, lefts, rights, dims, name)
            return sent, kept
        return multiply(False, core, lefts, rights, dims, name)[0]

    if paired:
        sent, kept = multiply(True, core, [hidden], [w_down], NN, "mlp_out")
        mlp_partial = [kept, swapped(sent)]
        sent, kept = multiply(True, core, [g_gate, g_up], [w_gate, w_up], NT, "norm2_grad")
        both = jnp.concatenate(
            [jnp.where(core[0] == 0, kept, sent), jnp.where(core[0] == 0, sent, kept)], axis=0
        )
        norm2_partial = [both, swapped(both)]
    else:
        part = multiply(False, core, [hidden], [w_down], NN, "mlp_out")[0]
        mlp_partial = [lax.psum_scatter(part, "narrow", scatter_dimension=0, tiled=True)]
        part = multiply(False, core, [g_gate, g_up], [w_gate, w_up], NT, "norm2_grad")[0]
        norm2_partial = [lax.psum(part, "narrow")]
    attn_own = own_of(jnp.concatenate(attn, axis=0))
    output, sums_out = output_rows(
        core, mlp_partial, frames, attn_own, output_grad, scale1, scale2
    )

    gh, gat, go, sums_middle = middle_back(
        core if paired else narrow.reshape(1) * 0,
        places,
        norm2_partial,
        x,
        attn,
        dy,
        scale1,
        gain2,
        w_out,
        rows_own if paired else length,
        piece,
    )
    if not paired:
        sums_middle = jnp.where(narrow == 0, sums_middle, 0.0)
    gq, gk, gv = attend_back(go, q, k, v, chances[0], chances[1], cos, sin, rows_per, span)
    ut = turn(places, u, piece)
    attention = wide.reduce(attention_weights(wide.fast, ut, gat, o, gq, gk, gv))
    attention = attention.reshape(piece, 4, heads)
    if paired:
        sent, kept = multiply(True, core, [gq, gk, gv], [w_query, w_key, w_value], NT, "norm1_grad")
        norm1_partial = [kept, swapped(sent)]
    else:
        part = multiply(False, core, [gq, gk, gv], [w_query, w_key, w_value], NT, "norm1_grad")[0]
        norm1_partial = [lax.psum_scatter(part, "narrow", scatter_dimension=0, tiled=True)]
    input_grad, sums_in = input_rows(norm1_partial, frames, own_of(gh), gain1)
    sums = lax.psum(sums_out + sums_middle + sums_in, ("wide", "narrow"))

    def gathered(at):
        return jnp.concatenate(
            [group[:, :, at].reshape(piece, -1) for group in groups], axis=1
        )

    return (
        output,
        input_grad,
        attention[:, 0],
        attention[:, 2],
        attention[:, 3],
        attention[:, 1].T,
        gathered(1),
        gathered(2),
        gathered(0).T,
        sums[4],
        sums[5],
        sums[0],
        sums[1],
        sums[2],
        sums[3],
    )


def solution(mesh):
    rows = P(("wide", "narrow"), None)
    across = P(None, "narrow")
    return jax.shard_map(
        on_device,
        mesh=mesh,
        in_specs=(rows, P("wide", None))
        + (across,) * 3
        + (P("narrow", None),)
        + (across,) * 2
        + (P("narrow", None),)
        + (P(),) * 6
        + (rows,),
        out_specs=(rows, rows)
        + (P("wide", "narrow"),) * 3
        + (P("narrow", "wide"),)
        + (P("wide", "narrow"),) * 2
        + (P("narrow", "wide"),)
        + (P(),) * 6,
        check_vma=False,
    )
```

time: 930 us -> 423 us (0.45)
  waiting for transfers between devices: 557 us -> 75.4 us
  matrix products: 154 us -> 0 us
  Pallas kernels: 0 us -> 154 us
  starting transfers between devices: 0.49 us -> 52.1 us
  other arithmetic: 67 us -> 33 us
  local copies, waits for them, and re-layouts: 74.3 us -> 58 us
  between operations: 15.1 us -> 2.12 us
  loops' own time: 11.3 us -> 0 us
    reduce_scatter x7 -> x0, waiting for transfers between devices: 445 us -> none  [the longest x1 95.3 us: on_device(): lax.psum_scatter(down_part.astype(jnp.bfloat16), 'wide', scatter_dimensio...]
    dot_general x35 -> x0, matrix products: 154 us -> none  [the longest x7 39.8 us: column_contract(): lax.dot_general(left_rows, right_rows, (((1,), (1,)), ((), ())), preferre...]
    pallas_call x0 -> x19, Pallas kernels: none -> 154 us  [the longest x4 49.3 us: feed(): call(functools.partial(feed_body, fast=fast, rows_per=min(rows_per, half)...]
    psum x3 -> x0, waiting for transfers between devices: 97.9 us -> none  [the longest x2 68.1 us: reduce_forward(): return lax.psum(partial_sum, 'narrow')]
    ppermute x0 -> x43, waiting for transfers between devices: none -> 75.4 us  [the longest x20 54.7 us: along(): lax.ppermute(values, 'wide', [(i, i ^ bit) for i in range(self.size)])]
    ppermute x0 -> x43, starting transfers between devices: none -> 52.1 us  [the longest x15 25.4 us: reduce(): lax.ppermute(both[shift * height:shift * height + height], 'wide', [(i, (...]
    dynamic_update_slice x4 -> x0, local copies, waits for them, and re-layouts: 41.2 us -> none  [attention_forward(): return lax.map(forward_block, jnp.arange(total_blocks, dtype=jnp.int32))]
    reduce_sum x11 -> x0, other arithmetic: 32.2 us -> none  [the longest x2 8.12 us: norm_back(): jnp.mean(scaled, axis=-1, keepdims=True)]
  transfers between devices with their start and end apart: 12 -> 43, of which waited for: 10 -> 13; matrix products, arithmetic and copies ran while one was open for 20% -> 15% of each run, Pallas kernels for 0% -> 24%
where the time goes in v1:
time: 423 us; the launch traced here: 414 us
  Pallas kernels  154 us (36%)
  waiting for transfers between devices  75.4 us (18%)
  local copies, waits for them, and re-layouts  58 us (14%)
  starting transfers between devices  52.1 us (12%)
  blocking collectives  39.9 us (9%)
  other arithmetic  33 us (8%)
    ppermute x20, waiting for transfers between devices, along(): lax.ppermute(values, 'wide', [(i, i ^ bit) for i in range(self.size)])  54.7 us
    pallas_call x4, Pallas kernels, feed(): call(functools.partial(feed_body, fast=fast, rows_per=min(rows_per, half)...  49.3 us
    psum x1, blocking collectives, on_device(): sums = lax.psum(sums_out + sums_middle + sums_in, ('wide', 'narrow'))  39.9 us
    unnamed x162, local copies, waits for them, and re-layouts  33 us
    pallas_call x3, Pallas kernels, multiply(): call(functools.partial(multiply_body, parts=len(lefts), dims=dims, own=ow...  29.3 us
    ppermute x15, starting transfers between devices, reduce(): lax.ppermute(both[shift * height:shift * height + height], 'wide', [(i, (...  25.4 us
    ppermute x20, starting transfers between devices, along(): lax.ppermute(values, 'wide', [(i, i ^ bit) for i in range(self.size)])  25 us
    ppermute x15, waiting for transfers between devices, reduce(): lax.ppermute(both[shift * height:shift * height + height], 'wide', [(i, (...  19 us
  transfers between devices with their start and end apart: 43, of which 13 were waited for; matrix products, arithmetic and copies ran while one was open for 15% of the time, Pallas kernels for 24%

profile of v1, /device:TPU:0, one launch (start us, length us, event | category | flops | bytes accessed | tf_op | source)
XLA Modules:
  0.0 414.2 jit_solution(4622866633095640314)
XLA Ops:
  9.6 8.9 %project.1 = (bf16[1024,512]{1,0:T(8,128)(2,1)S(1)}, bf16[1024,512]{1,0:T(8,128)(2,1)S(1)}, bf16[1024,512]{1,0:T(8,128)(2,1)S(1)}, bf16[1024,1024]{1,0:T(8,128)(...) custom-call(s32[1]{0:T(128)} %bitcast.core, bf16[512,1024]{1,0:T(8,128)(2,1)S(1)} %copy-done.5, ...), custom_call_target="tpu_custom_call" | custom-call | tf_op jit(solution)/shard_map/project/pallas_call | solution.py:156
  20.0 4.5 %attend.2 = (bf16[512,512]{1,0:T(8,128)(2,1)S(1)}, bf16[4,4,256,256]{3,2,1,0:T(8,128)(2,1)S(1)}) custom-call(bf16[1024,512]{1,0:T(8,128)(2,1)S(1)} %get-tuple-element.84.q, bf16[1024,512]{1,0:T(8,128)(2,1)S(1)} %get-tuple-element.85.k, bf16[1024,512]{1,0:T(8,128)(2,1)S(1)} %get-tuple-element.86.v, s32[1,1024]{1,0:T(1,128)S(1)} %copy-done.38, ...), custom_call_target="tpu_custom_call" | custom-call | tf_op jit(solution)/shard_map/attend/pallas_call | solution.py:241
  26.4 4.5 %attend.3 = (bf16[512,512]{1,0:T(8,128)(2,1)S(1)}, bf16[4,4,256,256]{3,2,1,0:T(8,128)(2,1)S(1)}) custom-call(bf16[1024,512]{1,0:T(8,128)(2,1)S(1)} %get-tuple-element.84.q, bf16[1024,512]{1,0:T(8,128)(2,1)S(1)} %get-tuple-element.85.k, bf16[1024,512]{1,0:T(8,128)(2,1)S(1)} %get-tuple-element.86.v, s32[1,1024]{1,0:T(1,128)S(1)} %copy-done.38, ...), custom_call_target="tpu_custom_call" | custom-call | tf_op jit(solution)/shard_map/attend/pallas_call | solution.py:241
  37.0 5.0 %cotangent.1 = (bf16[1024,1024]{1,0:T(8,128)(2,1)S(1)}, bf16[1024,1024]{1,0:T(8,128)(2,1)}, bf16[1024,1024]{1,0:T(8,128)(2,1)}) custom-call(s32[1]{0:T(128)} %bitcast.core, s32[16]{0:T(128)S(1)} %fusion.15.places, bf16[512,1024]{1,0:T(8,128)(2,1)S(1)} %copy-done.12, bf16[512,1024]{1,0:T(8,128)(2,1)} %collective-permute-done.4.other, f32[1,1024]{1,0:T(1,128)S(1)} %bitcast.70), custom_call_target="tpu_custom_call" | custom-call | tf_op jit(solution)/shard_map/cotangent/pallas_call | solution.py:354
  43.7 4.5 %middle.2 = (bf16[512,1024]{1,0:T(8,128)(2,1)S(1)}, bf16[512,1024]{1,0:T(8,128)(2,1)S(1)}, bf16[1024,512]{1,0:T(8,128)(2,1)S(1)}) custom-call(s32[16]{0:T(128)S(1)} %fusion.15.places, bf16[512,512]{1,0:T(8,128)(2,1)S(1)} %get-tuple-element.87.refs_0_, bf16[512,1024]{1,0:T(8,128)(2,1)S(1)} %copy-done.10, bf16[512,512]{1,0:T(8,128)(2,1)} %collective-permute-done.1.refs_2_, ...), custom_call_target="tpu_custom_call" | custom-call | tf_op jit(solution)/shard_map/middle/pallas_call | solution.py:420
  50.2 4.4 %middle.3 = (bf16[512,1024]{1,0:T(8,128)(2,1)S(1)}, bf16[512,1024]{1,0:T(8,128)(2,1)S(1)}, bf16[1024,512]{1,0:T(8,128)(2,1)S(1)}) custom-call(s32[16]{0:T(128)S(1)} %fusion.15.places, bf16[512,512]{1,0:T(8,128)(2,1)S(1)} %get-tuple-element.90.refs_0_, bf16[512,1024]{1,0:T(8,128)(2,1)S(1)} %copy-done.10, bf16[512,512]{1,0:T(8,128)(2,1)S(1)} %collective-permute-done.3.refs_2_, ...), custom_call_target="tpu_custom_call" | custom-call | tf_op jit(solution)/shard_map/middle/pallas_call | solution.py:420
  56.5 7.5 %feed.4 = (bf16[1024,256]{1,0:T(8,128)(2,1)}, bf16[1024,256]{1,0:T(8,128)(2,1)}, bf16[1024,256]{1,0:T(8,128)(2,1)}, bf16[512,384]{1,0:T(8,128)(2,1)S(1)}, bf16[5...) custom-call(bf16[512,1024]{1,0:T(8,128)(2,1)} %copy-done, ...), custom_call_target="tpu_custom_call" | custom-call | tf_op jit(solution)/shard_map/feed/pallas_call | solution.py:497
  64.1 12.8 %feed.6 = (bf16[1024,512]{1,0:T(8,128)(2,1)}, bf16[1024,512]{1,0:T(8,128)(2,1)}, bf16[1024,512]{1,0:T(8,128)(2,1)}, bf16[512,768]{1,0:T(8,128)(2,1)}, bf16[512,7...) custom-call(bf16[512,1024]{1,0:T(8,128)(2,1)} %copy-done, bf16[512,1024]{1,0:T(8,128)(2,1)} %copy-done.3, ...), custom_call_target="tpu_custom_call" | custom-call | tf_op jit(solution)/shard_map/feed/pallas_call | solution.py:497
  76.9 13.0 %feed.5 = (bf16[1024,512]{1,0:T(8,128)(2,1)}, bf16[1024,512]{1,0:T(8,128)(2,1)}, bf16[1024,512]{1,0:T(8,128)(2,1)}, bf16[512,768]{1,0:T(8,128)(2,1)}, bf16[512,7...) custom-call(bf16[512,1024]{1,0:T(8,128)(2,1)} %copy-done, bf16[512,1024]{1,0:T(8,128)(2,1)} %copy-done.3, ...), custom_call_target="tpu_custom_call" | custom-call | tf_op jit(solution)/shard_map/feed/pallas_call | solution.py:497
  90.0 15.9 %feed.7 = (bf16[1024,768]{1,0:T(8,128)(2,1)}, bf16[1024,768]{1,0:T(8,128)(2,1)}, bf16[1024,768]{1,0:T(8,128)(2,1)}, bf16[512,1152]{1,0:T(8,128)(2,1)}, bf16[512,...) custom-call(bf16[512,1024]{1,0:T(8,128)(2,1)S(1)} %copy-done.1, ...), custom_call_target="tpu_custom_call" | custom-call | tf_op jit(solution)/shard_map/feed/pallas_call | solution.py:497
  110.9 6.3 %pad_maximum_fusion = (bf16[1024,2048]{1,0:T(8,128)(2,1)}, bf16[1024,2048]{1,0:T(8,128)(2,1)}) fusion(bf16[1024,768]{1,0:T(8,128)(2,1)} %get-tuple-element.99, bf16[1024,512]{1,0:T(8,128)(2,1)S(1)} %copy-done.57, bf16[1024,512]{1,0:T(8,128)(2,1)S(1)} %copy-done.59, bf16[1024,256]{1,0:T(8,128)(2,1)S(1)} %copy-done.66, bf16[1024,768]{1,0:T(8,128)(2,1)} %get-tuple-element.108, ...), kind=kLoop, calls=%fused_computation | loop fusion | flops 33554432 | bytes 16777216 | tf_op jit(solution)/shard_map/concatenate | solution.py:861
  117.2 8.8 %mlp_out.1 = (bf16[512,1024]{1,0:T(8,128)(2,1)}, bf16[512,1024]{1,0:T(8,128)(2,1)S(1)}) custom-call(s32[1]{0:T(128)} %bitcast.core, bf16[1024,2048]{1,0:T(8,128)(2,1)} %get-tuple-element.205.refs_0_, bf16[2048,1024]{1,0:T(8,128)(2,1)} %refs_1_.5), custom_call_target="tpu_custom_call" | custom-call | tf_op jit(solution)/shard_map/mlp_out/pallas_call | solution.py:558
  128.5 14.0 %norm2_grad.1 = (bf16[512,1024]{1,0:T(8,128)(2,1)S(1)}, bf16[512,1024]{1,0:T(8,128)(2,1)S(1)}) custom-call(s32[1]{0:T(128)} %bitcast.core, bf16[1024,2048]{1,0:T(8,128)(2,1)} %get-tuple-element.206.refs_0_, bf16[1024,2048]{1,0:T(8,128)(2,1)} %pad_maximum_fusion.2.refs_1_, bf16[1024,2048]{1,0:T(8,128)(2,1)} %refs_2_.4, bf16[1024,2048]{1,0:T(8,128)(2,1)} %refs_3_.2), custom_call_target="tpu_custom_call" | custom-call | tf_op jit(solution)/shard_map/norm2_grad/pallas_call | solution.py:558
  174.4 8.4 %collective-permute-done.22 = bf16[512,768]{1,0:T(8,128)(2,1)} collective-permute-done((bf16[512,768]{1,0:T(8,128)(2,1)}, bf16[512,768]{1,0:T(8,128)(2,1)}, u32[]{:S(2)}, u32[]{:S(2)}) %collective-permute-start.22) | collective-permute-done | bytes 786464 | tf_op jit(solution)/shard_map/ppermute | solution.py:744
  197.4 27.9 %collective-permute-done.23 = bf16[256,768]{1,0:T(8,128)(2,1)S(1)} collective-permute-done((bf16[256,768]{1,0:T(8,128)(2,1)S(1)}, bf16[256,768]{1,0:T(8,128)(2,1)S(1)}, u32[]{:S(2)}, u32[]{:S(2)}) %collective-permute-start.23) | collective-permute-done | bytes 393248 | tf_op jit(solution)/shard_map/ppermute | solution.py:744
  245.3 8.3 %collective-permute-done.27 = bf16[64,1536]{1,0:T(8,128)(2,1)S(1)} collective-permute-done((bf16[64,1536]{1,0:T(8,128)(2,1)S(1)}, bf16[64,1536]{1,0:T(8,128)(2,1)S(1)}, u32[]{:S(2)}, u32[]{:S(2)}) %collective-permute-start.27) | collective-permute-done | bytes 196640 | tf_op jit(solution)/shard_map/ppermute | solution.py:759
  261.6 5.2 %collective-permute-start.40 = (bf16[64,2304]{1,0:T(8,128)(2,1)}, bf16[64,2304]{1,0:T(8,128)(2,1)}, u32[]{:S(2)}, u32[]{:S(2)}) collective-permute-start(bf16[64,2304]{1,0:T(8,128)(2,1)} %get-tuple-element.164), channel_id=1, source_target_pairs={{0,8},{2,10},{4,12},{6,14},{8,16},{10,18},{12,20},{14,22},{16,24},... | collective-permute-start | bytes 884744 | tf_op jit(solution)/shard_map/ppermute | solution.py:759
  266.8 4.2 %collective-permute-start.41 = (bf16[64,2304]{1,0:T(8,128)(2,1)}, bf16[64,2304]{1,0:T(8,128)(2,1)}, u32[]{:S(2)}, u32[]{:S(2)}) collective-permute-start(bf16[64,2304]{1,0:T(8,128)(2,1)} %get-tuple-element.166), channel_id=1, source_target_pairs={{0,16},{2,18},{4,20},{6,22},{8,24},{10,26},{12,28},{14,30},{16,0},... | collective-permute-start | bytes 884744 | tf_op jit(solution)/shard_map/ppermute | solution.py:759
  281.1 10.2 %middle_back.1 = (f32[1024,1024]{1,0:T(8,128)}, bf16[1024,1024]{1,0:T(8,128)(2,1)S(1)}, bf16[1024,512]{1,0:T(8,128)(2,1)S(1)}, f32[8,1024]{1,0:T(8,128)S(1)}) custom-call(s32[1]{0:T(128)} %bitcast.core, s32[16]{0:T(128)S(1)} %fusion.15.places, bf16[1024,1024]{1,0:T(8,128)(2,1)} %pad_maximum_fusion.3.refs_0_, ...), custom_call_target="tpu_custom_call" | custom-call | tf_op jit(solution)/shard_map/middle_back/pallas_call | solution.py:604
  292.7 17.9 %attend_back.1 = (bf16[1024,512]{1,0:T(8,128)(2,1)S(1)}, bf16[1024,512]{1,0:T(8,128)(2,1)S(1)}, bf16[1024,512]{1,0:T(8,128)(2,1)S(1)}) custom-call(bf16[1024,512]{1,0:T(8,128)(2,1)S(1)} %get-tuple-element.116.go, bf16[1024,512]{1,0:T(8,128)(2,1)} %copy-done.7, bf16[1024,512]{1,0:T(8,128)(2,1)} %copy-done.8, bf16[1024,512]{1,0:T(8,128)(2,1)} %copy-done.9, ...), custom_call_target="tpu_custom_call" | custom-call | tf_op jit(solution)/shard_map/attend_back/pallas_call | solution.py:305
  313.5 8.2 %attention_weights.1 = (bf16[512,1024]{1,0:T(8,128)(2,1)}, bf16[512,1024]{1,0:T(8,128)(2,1)S(1)}, bf16[512,1024]{1,0:T(8,128)(2,1)}, bf16[512,1024]{1,0:T(8,128)(2,1)S(1)}) custom-call(bf16[1024,1024]{1,0:T(8,128)(2,1)} %copy-done.11, bf16[1024,1024]{1,0:T(8,128)(2,1)} %copy-done.25, bf16[1024,512]{1,0:T(8,128)(2,1)S(1)} %copy-done.20, ...), custom_call_target="tpu_custom_call" | custom-call | tf_op jit(solution)/shard_map/attention_weights/pallas_call | solution.py:656
  336.2 6.5 %norm1_grad.1 = (bf16[512,1024]{1,0:T(8,128)(2,1)S(1)}, bf16[512,1024]{1,0:T(8,128)(2,1)S(1)}) custom-call(s32[1]{0:T(128)} %bitcast.core, bf16[1024,512]{1,0:T(8,128)(2,1)S(1)} %copy-done.15, bf16[1024,512]{1,0:T(8,128)(2,1)S(1)} %copy-done.17, bf16[1024,512]{1,0:T(8,128)(2,1)S(1)} %copy-done.19, bf16[1024,512]{1,0:T(8,128)(2,1)} %refs_3_.3, ...), custom_call_target="tpu_custom_call" | custom-call | tf_op jit(solution)/shard_map/norm1_grad/pallas_call | solution.py:558
  356.3 5.4 %collective-permute-done.9 = bf16[256,1024]{1,0:T(8,128)(2,1)S(1)} collective-permute-done((bf16[256,1024]{1,0:T(8,128)(2,1)S(1)}, bf16[256,1024]{1,0:T(8,128)(2,1)S(1)}, u32[]{:S(2)}, u32[]{:S(2)}) %collective-permute-start.9) | collective-permute-done | bytes 524320 | tf_op jit(solution)/shard_map/ppermute | solution.py:744
  369.6 39.9 %psum.7 = f32[8,1024]{1,0:T(8,128)S(1)} all-reduce(f32[8,1024]{1,0:T(8,128)S(1)} %add_add_fusion), channel_id=1, replica_groups=mesh['wide'=16,'narrow'=2] {'wide','narrow'}, use_global_device_ids=true, to_apply=%region_0.1 | all-reduce | flops 8192 | bytes 65536 | tf_op jit(solution)/shard_map/psum | solution.py:915
  (316 shorter events, 159.8 us)
Async XLA Ops:
  1.2 35.8 %collective-permute-start.4 = (bf16[512,1024]{1,0:T(8,128)(2,1)}, bf16[512,1024]{1,0:T(8,128)(2,1)}, u32[]{:S(2)}, u32[]{:S(2)}) collective-permute-start(bf16[512,1024]{1,0:T(8,128)(2,1)} %refs_4_.2), channel_id=1, source_target_pairs={{0,1},{1,0},{2,3},{3,2},{4,5},{5,4},{6,7},{7,6},{8,9},{9,8},{10,11... | collective-permute-start | bytes 3145736 | tf_op jit(solution)/shard_map/ppermute | solution.py:801
  1.2 41.9 %collective-permute-start.2 = (bf16[512,1024]{1,0:T(8,128)(2,1)}, bf16[512,1024]{1,0:T(8,128)(2,1)}, u32[]{:S(2)}, u32[]{:S(2)}) collective-permute-start(bf16[512,1024]{1,0:T(8,128)(2,1)} %refs_7_.1), channel_id=1, source_target_pairs={{0,1},{1,0},{2,3},{3,2},{4,5},{5,4},{6,7},{7,6},{8,9},{9,8},{10,11... | collective-permute-start | bytes 3145736 | tf_op jit(solution)/shard_map/ppermute | solution.py:801
  105.9 36.6 %collective-permute-start.15 = (bf16[512,384]{1,0:T(8,128)(2,1)S(1)}, bf16[512,384]{1,0:T(8,128)(2,1)S(1)}, u32[]{:S(2)}, u32[]{:S(2)}) collective-permute-start(bf16[512,384]{1,0:T(8,128)(2,1)S(1)} %get-tuple-element.135), channel_id=1, source_target_pairs={{0,2},{2,0},{4,6},{6,4},{8,10},{10,8},{12,14},{14,12},{16,18},{18,... | collective-permute-start | bytes 1179656 | tf_op jit(solution)/shard_map/ppermute | solution.py:744
  108.8 37.5 %collective-permute-start.17 = (bf16[512,384]{1,0:T(8,128)(2,1)S(1)}, bf16[512,384]{1,0:T(8,128)(2,1)S(1)}, u32[]{:S(2)}, u32[]{:S(2)}) collective-permute-start(bf16[512,384]{1,0:T(8,128)(2,1)S(1)} %get-tuple-element.137), channel_id=1, source_target_pairs={{0,4},{2,6},{4,0},{6,2},{8,12},{10,14},{12,8},{14,10},{16,20},{18,... | collective-permute-start | bytes 1179656 | tf_op jit(solution)/shard_map/ppermute | solution.py:744
  110.3 57.7 %collective-permute-start.29 = (bf16[512,768]{1,0:T(8,128)(2,1)}, bf16[512,768]{1,0:T(8,128)(2,1)}, u32[]{:S(2)}, u32[]{:S(2)}) collective-permute-start(bf16[512,768]{1,0:T(8,128)(2,1)} %get-tuple-element.143), channel_id=1, source_target_pairs={{0,2},{2,0},{4,6},{6,4},{8,10},{10,8},{12,14},{14,12},{16,18},{18,... | collective-permute-start | bytes 2359304 | tf_op jit(solution)/shard_map/ppermute | solution.py:744
  110.8 59.9 %collective-permute-start.31 = (bf16[512,768]{1,0:T(8,128)(2,1)}, bf16[512,768]{1,0:T(8,128)(2,1)}, u32[]{:S(2)}, u32[]{:S(2)}) collective-permute-start(bf16[512,768]{1,0:T(8,128)(2,1)} %get-tuple-element.145), channel_id=1, source_target_pairs={{0,4},{2,6},{4,0},{6,2},{8,12},{10,14},{12,8},{14,10},{16,20},{18,... | collective-permute-start | bytes 2359304 | tf_op jit(solution)/shard_map/ppermute | solution.py:744
  126.0 63.9 %collective-permute-start.5 = (bf16[512,1024]{1,0:T(8,128)(2,1)}, bf16[512,1024]{1,0:T(8,128)(2,1)}, u32[]{:S(2)}, u32[]{:S(2)}) collective-permute-start(bf16[512,1024]{1,0:T(8,128)(2,1)} %get-tuple-element.101), channel_id=1, source_target_pairs={{0,1},{1,0},{2,3},{3,2},{4,5},{5,4},{6,7},{7,6},{8,9},{9,8},{10,11... | collective-permute-start | bytes 3145736 | tf_op jit(solution)/shard_map/ppermute | solution.py:801
  161.9 20.9 %collective-permute-start.22 = (bf16[512,768]{1,0:T(8,128)(2,1)}, bf16[512,768]{1,0:T(8,128)(2,1)}, u32[]{:S(2)}, u32[]{:S(2)}) collective-permute-start(bf16[512,768]{1,0:T(8,128)(2,1)} %get-tuple-element.139), channel_id=1, source_target_pairs={{0,2},{2,0},{4,6},{6,4},{8,10},{10,8},{12,14},{14,12},{16,18},{18,... | collective-permute-start | bytes 2359304 | tf_op jit(solution)/shard_map/ppermute | solution.py:744
  169.6 26.0 %collective-permute-start.30 = (bf16[256,768]{1,0:T(8,128)(2,1)S(1)}, bf16[256,768]{1,0:T(8,128)(2,1)S(1)}, u32[]{:S(2)}, u32[]{:S(2)}) collective-permute-start(bf16[256,768]{1,0:T(8,128)(2,1)S(1)} %slice.340), channel_id=1, source_target_pairs={{0,4},{2,6},{4,0},{6,2},{8,12},{10,14},{12,8},{14,10},{16,20},{18,... | collective-permute-start | bytes 1179656 | tf_op jit(solution)/shard_map/ppermute | solution.py:744
  172.2 25.1 %collective-permute-start.32 = (bf16[256,768]{1,0:T(8,128)(2,1)S(1)}, bf16[256,768]{1,0:T(8,128)(2,1)S(1)}, u32[]{:S(2)}, u32[]{:S(2)}) collective-permute-start(bf16[256,768]{1,0:T(8,128)(2,1)S(1)} %slice.342), channel_id=1, source_target_pairs={{0,2},{2,0},{4,6},{6,4},{8,10},{10,8},{12,14},{14,12},{16,18},{18,... | collective-permute-start | bytes 1179656 | tf_op jit(solution)/shard_map/ppermute | solution.py:744
  182.8 45.1 %collective-permute-start.36 = (bf16[512,1152]{1,0:T(8,128)(2,1)}, bf16[512,1152]{1,0:T(8,128)(2,1)S(1)}, u32[]{:S(2)}, u32[]{:S(2)}) collective-permute-start(bf16[512,1152]{1,0:T(8,128)(2,1)} %get-tuple-element.147), channel_id=1, source_target_pairs={{0,2},{2,0},{4,6},{6,4},{8,10},{10,8},{12,14},{14,12},{16,18},{18,... | collective-permute-start | bytes 3538952 | tf_op jit(solution)/shard_map/ppermute | solution.py:744
  187.4 42.9 %collective-permute-start.38 = (bf16[512,1152]{1,0:T(8,128)(2,1)}, bf16[512,1152]{1,0:T(8,128)(2,1)S(1)}, u32[]{:S(2)}, u32[]{:S(2)}) collective-permute-start(bf16[512,1152]{1,0:T(8,128)(2,1)} %get-tuple-element.149), channel_id=1, source_target_pairs={{0,4},{2,6},{4,0},{6,2},{8,12},{10,14},{12,8},{14,10},{16,20},{18,... | collective-permute-start | bytes 3538952 | tf_op jit(solution)/shard_map/ppermute | solution.py:744
  189.9 35.4 %collective-permute-start.23 = (bf16[256,768]{1,0:T(8,128)(2,1)S(1)}, bf16[256,768]{1,0:T(8,128)(2,1)S(1)}, u32[]{:S(2)}, u32[]{:S(2)}) collective-permute-start(bf16[256,768]{1,0:T(8,128)(2,1)S(1)} %slice.329), channel_id=1, source_target_pairs={{0,4},{2,6},{4,0},{6,2},{8,12},{10,14},{12,8},{14,10},{16,20},{18,... | collective-permute-start | bytes 1179656 | tf_op jit(solution)/shard_map/ppermute | solution.py:744
  195.7 32.0 %collective-permute-start.25 = (bf16[256,768]{1,0:T(8,128)(2,1)S(1)}, bf16[256,768]{1,0:T(8,128)(2,1)S(1)}, u32[]{:S(2)}, u32[]{:S(2)}) collective-permute-start(bf16[256,768]{1,0:T(8,128)(2,1)S(1)} %slice.331), channel_id=1, source_target_pairs={{0,2},{2,0},{4,6},{6,4},{8,10},{10,8},{12,14},{14,12},{16,18},{18,... | collective-permute-start | bytes 1179656 | tf_op jit(solution)/shard_map/ppermute | solution.py:744
  197.3 36.7 %collective-permute-start.33 = (bf16[64,1536]{1,0:T(8,128)(2,1)S(1)}, bf16[64,1536]{1,0:T(8,128)(2,1)S(1)}, u32[]{:S(2)}, u32[]{:S(2)}) collective-permute-start(bf16[64,1536]{1,0:T(8,128)(2,1)S(1)} %get-tuple-element.173), channel_id=1, source_target_pairs={{0,8},{2,10},{4,12},{6,14},{8,16},{10,18},{12,20},{14,22},{16,24},... | collective-permute-start | bytes 589832 | tf_op jit(solution)/shard_map/ppermute | solution.py:759
  227.9 53.2 %collective-permute-start.6 = (bf16[1024,1024]{1,0:T(8,128)(2,1)}, bf16[1024,1024]{1,0:T(8,128)(2,1)}, u32[]{:S(2)}, u32[]{:S(2)}) collective-permute-start(bf16[1024,1024]{1,0:T(8,128)(2,1)} %pad_maximum_fusion.3.refs_0_), channel_id=1, source_target_pairs={{0,1},{1,0},{2,3},{3,2},{4,5},{5,4},{6,7},{7,6},{8,9},{9,8},{10,11... | collective-permute-start | bytes 6291464 | tf_op jit(solution)/shard_map/ppermute | solution.py:801
  261.6 64.0 %collective-permute-start.40 = (bf16[64,2304]{1,0:T(8,128)(2,1)}, bf16[64,2304]{1,0:T(8,128)(2,1)}, u32[]{:S(2)}, u32[]{:S(2)}) collective-permute-start(bf16[64,2304]{1,0:T(8,128)(2,1)} %get-tuple-element.164), channel_id=1, source_target_pairs={{0,8},{2,10},{4,12},{6,14},{8,16},{10,18},{12,20},{14,22},{16,24},... | collective-permute-start | bytes 884744 | tf_op jit(solution)/shard_map/ppermute | solution.py:759
  266.8 58.8 %collective-permute-start.42 = (bf16[64,2304]{1,0:T(8,128)(2,1)}, bf16[64,2304]{1,0:T(8,128)(2,1)}, u32[]{:S(2)}, u32[]{:S(2)}) collective-permute-start(bf16[64,2304]{1,0:T(8,128)(2,1)} %get-tuple-element.165), channel_id=1, source_target_pairs={{0,24},{2,26},{4,28},{6,30},{8,0},{10,2},{12,4},{14,6},{16,8},{18,... | collective-permute-start | bytes 884744 | tf_op jit(solution)/shard_map/ppermute | solution.py:759
  266.8 58.8 %collective-permute-start.41 = (bf16[64,2304]{1,0:T(8,128)(2,1)}, bf16[64,2304]{1,0:T(8,128)(2,1)}, u32[]{:S(2)}, u32[]{:S(2)}) collective-permute-start(bf16[64,2304]{1,0:T(8,128)(2,1)} %get-tuple-element.166), channel_id=1, source_target_pairs={{0,16},{2,18},{4,20},{6,22},{8,24},{10,26},{12,28},{14,30},{16,0},... | collective-permute-start | bytes 884744 | tf_op jit(solution)/shard_map/ppermute | solution.py:759
  323.6 21.9 %collective-permute-start.8 = (bf16[512,1024]{1,0:T(8,128)(2,1)}, bf16[512,1024]{1,0:T(8,128)(2,1)}, u32[]{:S(2)}, u32[]{:S(2)}) collective-permute-start(bf16[512,1024]{1,0:T(8,128)(2,1)} %get-tuple-element.131), channel_id=1, source_target_pairs={{0,2},{2,0},{4,6},{6,4},{8,10},{10,8},{12,14},{14,12},{16,18},{18,... | collective-permute-start | bytes 3145736 | tf_op jit(solution)/shard_map/ppermute | solution.py:744
  325.0 24.6 %collective-permute-start.10 = (bf16[512,1024]{1,0:T(8,128)(2,1)}, bf16[512,1024]{1,0:T(8,128)(2,1)}, u32[]{:S(2)}, u32[]{:S(2)}) collective-permute-start(bf16[512,1024]{1,0:T(8,128)(2,1)} %get-tuple-element.133), channel_id=1, source_target_pairs={{0,4},{2,6},{4,0},{6,2},{8,12},{10,14},{12,8},{14,10},{16,20},{18,... | collective-permute-start | bytes 3145736 | tf_op jit(solution)/shard_map/ppermute | solution.py:744
  365.8 44.4 %collective-permute-start.12 = (bf16[64,2048]{1,0:T(8,128)(2,1)S(1)}, bf16[64,2048]{1,0:T(8,128)(2,1)S(1)}, u32[]{:S(2)}, u32[]{:S(2)}) collective-permute-start(bf16[64,2048]{1,0:T(8,128)(2,1)S(1)} %get-tuple-element.167), channel_id=1, source_target_pairs={{0,8},{2,10},{4,12},{6,14},{8,16},{10,18},{12,20},{14,22},{16,24},... | collective-permute-start | bytes 786440 | tf_op jit(solution)/shard_map/ppermute | solution.py:759
  365.8 44.4 %collective-permute-start.14 = (bf16[64,2048]{1,0:T(8,128)(2,1)S(1)}, bf16[64,2048]{1,0:T(8,128)(2,1)S(1)}, u32[]{:S(2)}, u32[]{:S(2)}) collective-permute-start(bf16[64,2048]{1,0:T(8,128)(2,1)S(1)} %get-tuple-element.168), channel_id=1, source_target_pairs={{0,24},{2,26},{4,28},{6,30},{8,0},{10,2},{12,4},{14,6},{16,8},{18,... | collective-permute-start | bytes 786440 | tf_op jit(solution)/shard_map/ppermute | solution.py:759
  369.6 40.6 %collective-permute-start.13 = (bf16[64,2048]{1,0:T(8,128)(2,1)S(1)}, bf16[64,2048]{1,0:T(8,128)(2,1)S(1)}, u32[]{:S(2)}, u32[]{:S(2)}) collective-permute-start(bf16[64,2048]{1,0:T(8,128)(2,1)S(1)} %get-tuple-element.169), channel_id=1, source_target_pairs={{0,16},{2,18},{4,20},{6,22},{8,24},{10,26},{12,28},{14,30},{16,0},... | collective-permute-start | bytes 786440 | tf_op jit(solution)/shard_map/ppermute | solution.py:759
  (92 other events, 673.5 us)
